TPU v7x, 128 devices: a whole 4x4x4 slice. The times are simulated.
128 devices in a mesh: lat: 8 (over x, z_hi), lon: 16 (over y, z_lo, core).
Axes of the slice: x: 4, y: 4, z: 4 (z_hi: 2, z_lo: 2; z = z_hi * 2 + z_lo), core: 2. Of those that a mesh axis runs over, the one named last changes fastest.
Arguments:
- features: bfloat16 [128, 16, 128, 256], P(('lat', 'lon')), may hold values from -6 to 6
- offsets: float32 [2, 128, 16, 128], P(None, ('lat', 'lon')), may hold values from -1 to 1
- counts: int32 [128, 128], P(('lat', 'lon')), may hold values from 1 to 16, as said below
- cell_index: int32 [128, 16, 128], P(('lat', 'lon')), may hold values from 0 to 4095
- kernel: bfloat16 [3, 3, 256, 256], replicated, may hold values from -0.125 to 0.125
- conv_bias: float32 [256], replicated, may hold values from -3 to 3
- cotangent: bfloat16 [256, 2048, 256], P('lat', 'lon'), may hold values from -6 to 6
Outputs:
- encoded: bfloat16 [256, 2048, 256], P('lat', 'lon')
- weight_grad: float32 [3, 3, 256, 256], replicated
- bias_grad: float32 [256], replicated
- obs_grad: bfloat16 [128, 16, 128, 256], P(('lat', 'lon'))
Inputs may be any that keep to these rules, and one draw needn't show every extreme that they name: `counts`: each destination tile receives 16 live slots from every device in some draws; in every draw at least one tile does, and every device sends 16 live slots to some tile.
All inputs are finite; a program needn't handle non-finite values.
Results may differ from a plain program's by a relative error of at most 0.008.
Values may be sent and summed in bfloat16 or wider, within the bound.
A program may use at most 128 MiB of HBM per device.

v0:
```python
import math

import jax
import jax.numpy as jnp
from jax import lax
from jax.sharding import PartitionSpec as P


def padded_2(cells, sides, width):
    for axis, dim in sides:
        count = lax.axis_size(axis)
        head = lax.slice_in_dim(cells, 0, width, axis=dim)
        tail = lax.slice_in_dim(cells, cells.shape[dim] - width, cells.shape[dim], axis=dim)
        cells = jnp.concatenate(
            [
                lax.ppermute(tail, axis, [(i, (i + 1) % count) for i in range(count)]),
                cells,
                lax.ppermute(head, axis, [((i + 1) % count, i) for i in range(count)]),
            ],
            axis=dim,
        )
    return cells


def close_poles(padded, margin):
    band = lax.axis_index("lat")
    bands = lax.axis_size("lat")
    row_ids = jnp.arange(padded.shape[0], dtype=jnp.int32)
    upper = (row_ids < margin) & (band == 0)
    lower = (row_ids >= padded.shape[0] - margin) & (band == bands - 1)
    keep = jnp.logical_not(upper | lower)
    return jnp.where(keep[:, None, None], padded, jnp.zeros_like(padded))


def column_views(padded, cols):
    return [padded[:, shift : shift + cols] for shift in range(3)]


def convolve(views, kernel, rows):
    channels = views[0].shape[2]
    cols = views[0].shape[1]
    total = jnp.zeros((rows * cols, kernel.shape[3]), jnp.float32)
    for row_off in range(3):
        for col_off in range(3):
            window = views[col_off][row_off : row_off + rows].reshape(-1, channels)
            total = total + jnp.dot(
                window, kernel[row_off, col_off], preferred_element_type=jnp.float32
            )
    return total.reshape(rows, cols, -1)


def back_convolve(views, kernel, rows):
    channels = views[0].shape[2]
    cols = views[0].shape[1]
    total = jnp.zeros((rows * cols, kernel.shape[2]), jnp.float32)
    for row_off in range(3):
        for col_off in range(3):
            window = views[2 - col_off][2 - row_off : 2 - row_off + rows].reshape(-1, channels)
            total = total + lax.dot_general(
                window,
                kernel[row_off, col_off],
                (((1,), (1,)), ((), ())),
                preferred_element_type=jnp.float32,
            )
    return total.reshape(rows, cols, -1)


def act_gradient(cotangent, activation):
    sigmoid_gate = jax.nn.sigmoid(activation)
    return (
        cotangent.astype(jnp.float32) * sigmoid_gate * (1.0 + activation * (1.0 - sigmoid_gate))
    ).astype(jnp.bfloat16)


def body(features, offsets, counts, cell_index, kernel, conv_bias, cotangent):
    slot_count = features.shape[1]
    devices = features.shape[2]
    channels = features.shape[3]
    rows_here = cotangent.shape[0]
    cols_here = cotangent.shape[1]
    n_lat = lax.axis_size("lat")
    n_lon = lax.axis_size("lon")
    slot_ids = jnp.arange(slot_count, dtype=jnp.int32)
    live_mask = slot_ids[:, None] < counts[0][None, :]
    radius = offsets[0, 0] * offsets[0, 0] + offsets[1, 0] * offsets[1, 0]
    weights = jnp.where(live_mask, jnp.exp(-2.0 * radius), 0.0).astype(jnp.bfloat16)
    outgoing = features[0]
    places = cell_index[0]
    received = (
        lax.all_to_all(outgoing, ("lat", "lon"), split_axis=1, concat_axis=1, tiled=True),
        lax.all_to_all(weights, ("lat", "lon"), split_axis=1, concat_axis=1, tiled=True),
        lax.all_to_all(places, ("lat", "lon"), split_axis=1, concat_axis=1, tiled=True),
    )
    in_features = received[0].reshape(-1, channels)
    weight_f32 = received[1].reshape(-1).astype(jnp.float32)
    in_places = received[2].reshape(-1)
    cell_total = rows_here * cols_here
    block_size = math.gcd(cell_total, 512)
    block_starts = jnp.arange(cell_total // block_size, dtype=jnp.int32) * block_size

    def splat_block(start):
        targets = start + jnp.arange(block_size, dtype=jnp.int32)
        spread = jnp.where(in_places[None, :] == targets[:, None], weight_f32[None, :], 0.0)
        summed = jnp.dot(
            spread.astype(jnp.bfloat16), in_features, preferred_element_type=jnp.float32
        )
        return (summed, jnp.sum(spread, axis=1))

    gathered, density = lax.map(splat_block, block_starts)
    gathered = gathered.reshape(cell_total, channels)
    density = density.reshape(cell_total)
    grid_field = (
        (gathered / (density[:, None] + 1.0))
        .astype(jnp.bfloat16)
        .reshape(rows_here, cols_here, channels)
    )
    padded = close_poles(padded_2(grid_field, (("lat", 0), ("lon", 1)), 1), 1)
    field_views = column_views(padded, cols_here)
    activation = convolve(field_views, kernel, rows_here) + conv_bias
    grad_act = act_gradient(cotangent, activation)
    grad_padded = close_poles(padded_2(grad_act, (("lat", 0), ("lon", 1)), 1), 1)
    encoded = (grid_field.astype(jnp.float32) + activation * jax.nn.sigmoid(activation)).astype(
        jnp.bfloat16
    )
    grad_flat = grad_act.reshape(-1, channels)
    blocks = []
    for row_off in range(3):
        for col_off in range(3):
            window = field_views[col_off][row_off : row_off + rows_here].reshape(-1, channels)
            blocks.append(
                lax.dot_general(
                    window, grad_flat, (((0,), (0,)), ((), ())), preferred_element_type=jnp.float32
                )
            )
    local_weight = jnp.stack(blocks).reshape(3, 3, channels, channels)
    local_bias = jnp.sum(grad_flat.astype(jnp.float32), axis=0)
    weight_sum, bias_sum = lax.psum((local_weight, local_bias), ("lat", "lon"))
    norm_scale = 1.0 / math.sqrt(cell_total * n_lat * n_lon)
    field_grad = cotangent.astype(jnp.float32) + back_convolve(
        column_views(grad_padded, cols_here), kernel, rows_here
    )
    scaled = (field_grad.reshape(-1, channels) / (density[:, None] + 1.0)).astype(jnp.bfloat16)
    picked = jnp.take(scaled, in_places, axis=0).astype(jnp.float32)
    slot_grads = (weight_f32[:, None] * picked).astype(jnp.bfloat16)
    returned_grads = lax.all_to_all(
        slot_grads.reshape(slot_count, devices, channels),
        ("lat", "lon"),
        split_axis=1,
        concat_axis=1,
        tiled=True,
    )
    obs_grad = returned_grads.reshape(1, slot_count, devices, channels)
    return (encoded, weight_sum * norm_scale, bias_sum * norm_scale, obs_grad)


def solution(mesh):
    return jax.shard_map(
        body,
        mesh=mesh,
        in_specs=(
            P(("lat", "lon"), None, None, None),
            P(None, ("lat", "lon"), None, None),
            P(("lat", "lon"), None),
            P(("lat", "lon"), None, None),
            P(),
            P(),
            P("lat", "lon", None),
        ),
        out_specs=(P("lat", "lon", None), P(), P(), P(("lat", "lon"), None, None, None)),
        check_vma=False,
    )
```

profile of v0, /device:TPU:1, one launch (start us, length us, event | category | flops | bytes accessed | tf_op | source)
XLA Modules:
  0.0 450.0 jit_solution(2705655743778766568)
XLA Ops:
  8.7 11.5 %all-to-all-start.1 = ((bf16[16,128,1]{0,2,1:T(2,128)(2,1)}), bf16[16,128,1]{0,2,1:T(2,128)(2,1)S(1)}, u32[]{:S(2)}, u32[]{:S(2)}) async-start(bf16[16,128,1]{0,2,1:T(2,128)(2,1)} %copy.226), calls=%async_computation.1 | async-start | bytes 131072 | tf_op jit(solution)/shard_map/all_to_all | solution.py:91
  21.7 8.2 %all-to-all-done.1 = bf16[16,128,1]{0,2,1:T(2,128)(2,1)S(1)} async-done(((bf16[16,128,1]{0,2,1:T(2,128)(2,1)}), bf16[16,128,1]{0,2,1:T(2,128)(2,1)S(1)}, u32[]{:S(2)}, u32[]{:S(2)}) %all-to-all-start.1) | async-done | bytes 4128 | tf_op jit(solution)/shard_map/all_to_all | solution.py:91
  29.9 4.1 all-to-all-start
  34.1 2.8 copy.295
  36.9 7.0 %all-to-all-done = s32[16,128,1]{0,2,1:T(1,128)S(1)} async-done(((s32[16,128,1]{0,2,1:T(1,128)}), s32[16,128,1]{0,2,1:T(1,128)S(1)}, u32[]{:S(2)}, u32[]{:S(2)}) %all-to-all-start) | async-done | bytes 8224 | tf_op jit(solution)/shard_map/all_to_all | solution.py:92
  43.8 4.1 all-to-all-start.2
  48.1 2.9 copy.247
  52.6 14.7 %all-to-all-done.2 = bf16[16,128,256]{2,0,1:T(8,128)(2,1)S(1)} async-done(((bf16[16,128,256]{2,0,1:T(8,128)(2,1)}), bf16[16,128,256]{2,0,1:T(8,128)(2,1)S(1)}, u32[]{:S(2)}, u32[]{:S(2)}) %all-to-all-start.2) | async-done | bytes 1048608 | tf_op jit(solution)/shard_map/all_to_all | solution.py:90
  67.7 27.4 %while.12 = (s32[]{:T(128)}, f32[8,512,256]{2,1,0:T(8,128)}, f32[8,512]{1,0:T(8,128)S(1)}, s32[16,128]{1,0:T(8,128)S(1)}, s32[8]{0:T(128)S(1)}, /*index=5*/f32[2...) while((s32[]{:T(128)}, f32[8,512,256]{2,1,0:T(8,128)}, f32[8,512]{1,0:T(8,128)S(1)}, ...), condition=%wide.region_2.3_spmd, body=%wide.region_0.2_spmd.sunk | while | flops 542113792 | bytes 1618045 | solution.py:109
  95.1 5.7 %copy.287 = f32[4096,256]{0,1:T(8,128)} copy(f32[4096,256]{1,0:T(8,128)} %bitcast.193) | data formatting | bytes 8388608 | tf_op jit(solution)/shard_map/reshape | solution.py:110
  100.8 2.5 divide_convert_fusion
  104.6 5.7 %copy.231 = f32[32,128,256]{1,2,0:T(8,128)} copy(f32[32,128,256]{2,1,0:T(8,128)} %bitcast.194) | data formatting | bytes 8388608 | tf_op jit(solution)/shard_map/reshape | solution.py:110
  112.1 2.7 divide_convert_fusion.1
  114.8 2.2 collective-permute-done
  117.3 3.0 fusion.74
  120.3 2.2 copy.234
  122.5 2.9 collective-permute-start.3
  125.4 2.2 copy.233
  130.4 2.0 copy.235
  132.4 8.0 %maximum_select_fusion = bf16[34,130,256]{1,2,0:T(8,128)(2,1)} fusion(bf16[34,1,256]{1,2,0:T(8,128)(2,1)} %copy.236, bf16[1,128,256]{1,2,0:T(8,128)(2,1)S(1)} %collective-permute-done.1, bf16[32,128,256]{1,2,0:T(8,128)(2,1)S(1)} %divide_convert_fusion.1, bf16[1,128,256]{1,2,0:T(8,128)(2,1)S(1)} %collective-permute-done, bf16[34,1,256]{1,2,0:T(8,128)(2,1)} %copy.235, ...), kind=kLoop, calls=%fused_computation.30 | loop fusion | flops 12446720 | bytes 4526114 | tf_op jit(solution)/shard_map/jit(_where)/select_n | solution.py:32
  140.4 19.6 %fusion.72 = (bf16[32,128,256]{1,2,0:T(8,128)(2,1)}, bf16[32,128,256]{1,2,0:T(8,128)(2,1)}, bf16[32,128,256]{1,2,0:T(8,128)(2,1)}, bf16[32,128,256]{1,2,0:T(8,12...) fusion(bf16[34,130,256]{1,2,0:T(8,128)(2,1)} %maximum_select_fusion), kind=kLoop, calls=%fused_computation.130 | loop fusion | bytes 37748736 | tf_op jit(solution)/shard_map/slice | solution.py:45
  159.9 3.3 copy.237
  163.2 4.1 copy.238
  167.3 4.1 copy.239
  171.4 4.1 copy.240
  175.5 4.1 copy.241
  179.6 4.1 copy.242
  183.7 4.1 copy.243
  187.8 4.1 copy.244
  191.9 4.7 %copy.245 = bf16[32,128,256]{2,1,0:T(8,128)(2,1)} copy(bf16[32,128,256]{1,2,0:T(8,128)(2,1)} %get-tuple-element.121) | data formatting | bytes 4194304 | tf_op jit(solution)/shard_map/slice | solution.py:45
  209.3 2.6 convolution_add_fusion.8
  211.9 5.7 %copy.246 = f32[32,128,256]{1,2,0:T(8,128)} copy(f32[32,128,256]{2,1,0:T(8,128)} %bitcast.195) | data formatting | bytes 8388608 | tf_op jit(solution)/shard_map/reshape | solution.py:49
  217.6 7.5 %convert_reduce_fusion = (f32[256]{0:T(256)}, bf16[32,128,256]{1,2,0:T(8,128)(2,1)S(1)}, bf16[32,128,256]{1,2,0:T(8,128)(2,1)}) fusion(f32[32,128,256]{1,2,0:T(8,128)} %copy.246, f32[256]{0:T(256)} %param.14, bf16[32,128,256]{1,2,0:T(8,128)(2,1)} %copy.247, f32[32,128,256]{1,2,0:T(8,128)} %copy.231, f32[32,128]{1,0:T(8,128)} %copy-done.29), kind=kLoop, calls=%fused_computation.37 | loop fusion | flops 19922688 | bytes 14698496 | tf_op jit(solution)/shard_map/reduce_sum | solution.py:136
  231.6 2.7 collective-permute-start.4
  239.3 3.0 fusion.73
  242.3 2.2 copy.259
  244.4 4.3 collective-permute-start.7
  248.7 2.2 copy.258
  251.0 3.9 fusion.12
  254.9 2.2 copy.261
  257.1 2.0 copy.260
  259.1 8.2 %maximum_select_fusion.1 = bf16[34,130,256]{1,2,0:T(8,128)(2,1)} fusion(bf16[34,1,256]{1,2,0:T(8,128)(2,1)} %copy.261, bf16[1,128,256]{1,2,0:T(8,128)(2,1)S(1)} %copy-done.25, bf16[32,128,256]{1,2,0:T(8,128)(2,1)S(1)} %get-tuple-element.111, bf16[1,128,256]{1,2,0:T(8,128)(2,1)S(1)} %copy-done.27, bf16[34,1,256]{1,2,0:T(8,128)(2,1)} %copy.260, ...), kind=kLoop, calls=%fused_computation.31 | loop fusion | flops 12446720 | bytes 4526114 | tf_op jit(solution)/shard_map/jit(_where)/select_n | solution.py:32
  267.3 20.1 %fusion.71 = (bf16[32,128,256]{1,2,0:T(8,128)(2,1)}, bf16[32,128,256]{1,2,0:T(8,128)(2,1)}, bf16[32,128,256]{1,2,0:T(8,128)(2,1)}, bf16[32,128,256]{1,2,0:T(8,12...) fusion(bf16[34,130,256]{1,2,0:T(8,128)(2,1)} %maximum_select_fu, ...), kind=kLoop, calls=%fused_computation.129 | loop fusion | bytes 37748736 | tf_op jit(solution)/shard_map/slice | solution.py:58
  287.4 3.3 copy.262
  290.7 2.7 fusion.37
  293.4 4.3 copy.263
  297.7 2.9 copy.264
  300.6 4.3 copy.265
  304.9 2.9 copy.266
  307.8 4.2 copy.267
  312.1 2.9 copy.268
  315.0 4.2 copy.269
  319.2 3.1 copy.270
  322.3 3.7 convolution_add_fusion.7
  335.7 2.8 convolution_add_fusion
  338.4 5.7 %copy.271 = f32[32,128,256]{1,2,0:T(8,128)} copy(f32[32,128,256]{2,1,0:T(8,128)} %bitcast.196) | data formatting | bytes 8388608 | tf_op jit(solution)/shard_map/reshape | solution.py:65
  344.2 4.1 fusion.11
  348.3 3.3 copy.274
  351.6 7.5 %gather_fusion = bf16[2048,256]{1,0:T(8,128)(2,1)S(1)} fusion(bf16[4096,256]{1,0:T(8,128)(2,1)S(1)} %copy.274, s32[2048]{0:T(1024)S(1)} %copy-done.31), kind=kCustom, calls=%fused_computation | custom fusion | bytes 2105344 | tf_op jit(solution)/shard_map/jit(_take)/gather | solution.py:143
  359.1 2.7 multiply_convert_fusion
  361.8 4.7 %all-to-all-start.3 = ((bf16[16,128,256]{2,0,1:T(8,128)(2,1)}), bf16[16,128,256]{2,0,1:T(8,128)(2,1)S(1)}, u32[]{:S(2)}, u32[]{:S(2)}) async-start(bf16[16,128,256]{2,0,1:T(8,128)(2,1)} %multiply_convert_fusion), calls=%async_computation.3 | async-start | bytes 2097152 | tf_op jit(solution)/shard_map/all_to_all | solution.py:145
  366.5 2.9 copy.276
  369.4 68.2 %psum.15 = f32[256]{0:T(256)S(1)} all-reduce(f32[256]{0:T(256)S(1)} %copy-done.32), channel_id=1, replica_groups=mesh['lat'=8,'lon'=16] {'lat','lon'}, use_global_device_ids=true, to_apply=%region_5.6 | all-reduce | flops 256 | bytes 2048 | tf_op jit(solution)/shard_map/psum | solution.py:137
  439.5 3.3 broadcast_multiply_fusion
  (179 shorter events, 74.0 us)
Async XLA Ops:
  8.7 21.3 %all-to-all-start.1 = ((bf16[16,128,1]{0,2,1:T(2,128)(2,1)}), bf16[16,128,1]{0,2,1:T(2,128)(2,1)S(1)}, u32[]{:S(2)}, u32[]{:S(2)}) async-start(bf16[16,128,1]{0,2,1:T(2,128)(2,1)} %copy.226), calls=%async_computation.1 | async-start | bytes 131072 | tf_op jit(solution)/shard_map/all_to_all | solution.py:91
  20.2 27.9 %copy-start.23 = (bf16[32,128,256]{2,1,0:T(8,128)(2,1)S(1)}, bf16[32,128,256]{2,1,0:T(8,128)(2,1)}, u32[]{:S(2)}) copy-start(bf16[32,128,256]{2,1,0:T(8,128)(2,1)} %param.15) | copy-start | bytes 6291460
  29.9 13.9 %all-to-all-start = ((s32[16,128,1]{0,2,1:T(1,128)}), s32[16,128,1]{0,2,1:T(1,128)S(1)}, u32[]{:S(2)}, u32[]{:S(2)}) async-start(s32[16,128,1]{0,2,1:T(1,128)} %bitcast.4), calls=%async_computation | async-start | bytes 131072 | tf_op jit(solution)/shard_map/all_to_all | solution.py:92
  43.8 23.5 %all-to-all-start.2 = ((bf16[16,128,256]{2,0,1:T(8,128)(2,1)}), bf16[16,128,256]{2,0,1:T(8,128)(2,1)S(1)}, u32[]{:S(2)}, u32[]{:S(2)}) async-start(bf16[16,128,256]{2,0,1:T(8,128)(2,1)} %bitcast.180), calls=%async_computation.2 | async-start | bytes 2097152 | tf_op jit(solution)/shard_map/all_to_all | solution.py:90
  48.0 391.5 %all-reduce.2.cloned.1.call-start = ((), (), s32[]{:S(2)}) async-start(), calls=%async_computation.4 | async-start | bytes 4718592 | tf_op jit(solution)/shard_map/psum | solution.py:137
  51.0 81.4 %copy-start.33 = (pred[34]{0:T(512)(128)(4,1)}, pred[34]{0:T(512)(128)(4,1)S(1)}, u32[]{:S(2)}) copy-start(pred[34]{0:T(512)(128)(4,1)S(1)} %or_not_fusion) | copy-start | bytes 106
  103.3 11.4 %collective-permute-start.1 = (bf16[1,128,256]{1,2,0:T(8,128)(2,1)S(1)}, bf16[1,128,256]{1,2,0:T(8,128)(2,1)S(1)}, u32[]{:S(2)}, u32[]{:S(2)}) collective-permute-start(bf16[1,128,256]{1,2,0:T(8,128)(2,1)S(1)} %get-tuple-element.138), channel_id=1, source_target_pairs={{16,0},{32,16},{48,32},{64,48},{80,64},{96,80},{112,96},{0,112},{1... | collective-permute-start | bytes 196616 | tf_op jit(solution)/shard_map/ppermute | solution.py:18
  110.3 4.5 %copy-start.29 = (f32[32,128]{1,0:T(8,128)}, f32[32,128]{1,0:T(8,128)S(1)}, u32[]{:S(2)}) copy-start(f32[32,128]{1,0:T(8,128)S(1)} %add.137) | copy-start | bytes 49156
  110.3 6.7 %collective-permute-start = (bf16[1,128,256]{1,2,0:T(8,128)(2,1)S(1)}, bf16[1,128,256]{1,2,0:T(8,128)(2,1)S(1)}, u32[]{:S(2)}, u32[]{:S(2)}) collective-permute-start(bf16[1,128,256]{1,2,0:T(8,128)(2,1)S(1)} %get-tuple-element.137), channel_id=1, source_target_pairs={{0,16},{16,32},{32,48},{48,64},{64,80},{80,96},{96,112},{112,0},{1... | collective-permute-start | bytes 196616 | tf_op jit(solution)/shard_map/ppermute | solution.py:16
  122.5 6.1 %collective-permute-start.3 = (bf16[34,1,256]{2,0,1:T(8,128)(2,1)S(1)}, bf16[34,1,256]{2,0,1:T(8,128)(2,1)S(1)}, u32[]{:S(2)}, u32[]{:S(2)}) collective-permute-start(bf16[34,1,256]{2,0,1:T(8,128)(2,1)S(1)} %copy.234), channel_id=1, source_target_pairs={{1,0},{2,1},{3,2},{4,3},{5,4},{6,5},{7,6},{8,7},{9,8},{10,9},{11,1... | collective-permute-start | bytes 52232 | tf_op jit(solution)/shard_map/ppermute | solution.py:18
  127.6 2.8 collective-permute-start.2
  191.9 4.7 %copy-start.21 = (bf16[3,3,256,256]{3,2,1,0:T(8,128)(2,1)S(1)}, bf16[3,3,256,256]{3,2,1,0:T(8,128)(2,1)}, u32[]{:S(2)}) copy-start(bf16[3,3,256,256]{3,2,1,0:T(8,128)(2,1)} %param.13) | copy-start | bytes 3538948
  196.6 1.6 copy-start.18
  198.1 1.6 copy-start.16
  199.7 1.6 copy-start.14
  201.3 1.6 copy-start.12
  202.9 1.6 copy-start.9
  204.5 1.6 copy-start.8
  206.1 1.6 copy-start.6
  207.7 1.6 copy-start.7
  211.9 13.1 %slice-start = ((s8[4456448]{0:T(1024)(128)(4,1)}), s8[262144]{0:T(1024)(128)(4,1)S(1)}, s32[]{:S(2)}) async-start(s8[4456448]{0:T(1024)(128)(4,1)} %bitcast.191), calls=%async_computation.5 | async-start | bytes 524288
  217.6 7.5 %slice-start.1 = ((s8[4456448]{0:T(1024)(128)(4,1)}), s8[4194304]{0:T(1024)(128)(4,1)S(1)}, s32[]{:S(2)}) async-start(s8[4456448]{0:T(1024)(128)(4,1)} %bitcast.191), calls=%async_computation.6 | async-start | bytes 8388608
  231.3 4.7 %collective-permute-start.5 = (bf16[1,128,256]{1,2,0:T(8,128)(2,1)S(1)}, bf16[1,128,256]{1,2,0:T(8,128)(2,1)S(1)}, u32[]{:S(2)}, u32[]{:S(2)}) collective-permute-start(bf16[1,128,256]{1,2,0:T(8,128)(2,1)S(1)} %get-tuple-element.136), channel_id=1, source_target_pairs={{16,0},{32,16},{48,32},{64,48},{80,64},{96,80},{112,96},{0,112},{1... | collective-permute-start | bytes 196616 | tf_op jit(solution)/shard_map/ppermute | solution.py:18
  231.6 6.7 %collective-permute-start.4 = (bf16[1,128,256]{1,2,0:T(8,128)(2,1)S(1)}, bf16[1,128,256]{1,2,0:T(8,128)(2,1)S(1)}, u32[]{:S(2)}, u32[]{:S(2)}) collective-permute-start(bf16[1,128,256]{1,2,0:T(8,128)(2,1)S(1)} %get-tuple-element.135), channel_id=1, source_target_pairs={{0,16},{16,32},{32,48},{48,64},{64,80},{80,96},{96,112},{112,0},{1... | collective-permute-start | bytes 196616 | tf_op jit(solution)/shard_map/ppermute | solution.py:16
  235.3 1.4 copy-start.22
  236.7 1.7 copy-start.24
  238.3 0.6 copy-start.26
  244.4 10.5 %collective-permute-start.7 = (bf16[34,1,256]{2,0,1:T(8,128)(2,1)S(1)}, bf16[34,1,256]{2,0,1:T(8,128)(2,1)S(1)}, u32[]{:S(2)}, u32[]{:S(2)}) collective-permute-start(bf16[34,1,256]{2,0,1:T(8,128)(2,1)S(1)} %copy.259), channel_id=1, source_target_pairs={{1,0},{2,1},{3,2},{4,3},{5,4},{6,5},{7,6},{8,7},{9,8},{10,9},{11,1... | collective-permute-start | bytes 52232 | tf_op jit(solution)/shard_map/ppermute | solution.py:18
  250.9 6.2 %collective-permute-start.6 = (bf16[34,1,256]{2,0,1:T(8,128)(2,1)S(1)}, bf16[34,1,256]{2,0,1:T(8,128)(2,1)S(1)}, u32[]{:S(2)}, u32[]{:S(2)}) collective-permute-start(bf16[34,1,256]{2,0,1:T(8,128)(2,1)S(1)} %copy.258), channel_id=1, source_target_pairs={{0,1},{1,2},{2,3},{3,4},{4,5},{5,6},{6,7},{7,8},{8,9},{9,10},{10,1... | collective-permute-start | bytes 52232 | tf_op jit(solution)/shard_map/ppermute | solution.py:16
  254.9 4.3 copy-start.25
  254.9 4.2 copy-start.27
  254.9 4.2 copy-start.34
  293.4 4.3 copy-start.5
  300.6 4.3 copy-start.4
  307.8 4.3 copy-start.3
  315.0 4.2 copy-start.2
  322.3 3.7 copy-start.20
  326.1 1.6 copy-start.19
  327.7 1.6 copy-start.17
  329.3 1.6 copy-start.15
  330.9 1.6 copy-start.13
  332.5 1.6 copy-start.10
  334.1 1.6 copy-start.11
  338.4 5.7 %copy-start = (bf16[32,128,256]{1,2,0:T(8,128)(2,1)S(1)}, bf16[32,128,256]{1,2,0:T(8,128)(2,1)}, u32[]{:S(2)}) copy-start(bf16[32,128,256]{1,2,0:T(8,128)(2,1)} %copy.247) | copy-start | bytes 6291460
  348.3 3.3 copy-start.31
  351.6 7.5 %copy-start.28 = (f32[16,128]{0,1:T(8,128)S(1)}, f32[16,128]{0,1:T(8,128)}, u32[]{:S(2)}) copy-start(f32[16,128]{0,1:T(8,128)} %copy.257) | copy-start | bytes 24580
  351.6 7.5 %copy-start.30 = (pred[16,128]{0,1:T(8,128)(4,1)S(1)}, pred[16,128]{0,1:T(8,128)(4,1)}, u32[]{:S(2)}) copy-start(pred[16,128]{0,1:T(8,128)(4,1)} %compare_and_fusion) | copy-start | bytes 6148
  359.1 7.4 %copy-start.1 = (bf16[32,128,256]{1,2,0:T(8,128)(2,1)S(1)}, bf16[32,128,256]{1,2,0:T(8,128)(2,1)}, u32[]{:S(2)}) copy-start(bf16[32,128,256]{1,2,0:T(8,128)(2,1)} %get-tuple-element.130) | copy-start | bytes 6291460
  361.8 76.4 %all-to-all-start.3 = ((bf16[16,128,256]{2,0,1:T(8,128)(2,1)}), bf16[16,128,256]{2,0,1:T(8,128)(2,1)S(1)}, u32[]{:S(2)}, u32[]{:S(2)}) async-start(bf16[16,128,256]{2,0,1:T(8,128)(2,1)} %multiply_convert_fusion), calls=%async_computation.3 | async-start | bytes 2097152 | tf_op jit(solution)/shard_map/all_to_all | solution.py:145
  366.5 2.9 copy-start.32
Sparse Core Ops, SparseCore 0:
  255.0 148.7 all-reduce.1
where the time goes:
time: 459 us; the launch traced here: 450 us
  local copies, waits for them, and re-layouts  197 us (43%)
  blocking collectives  68.2 us (15%)
  other arithmetic  51.6 us (11%)
  matrix products  45.3 us (10%)
  starting transfers between devices  38.2 us (8%)
  waiting for transfers between devices  34.4 us (7%)
  between operations  15.1 us (3%)
    psum x1, blocking collectives, body(): weight_sum, bias_sum = lax.psum((local_weight, local_bias), ('lat', 'lon'))  68.2 us
    slice x10, local copies, waits for them, and re-layouts, convolve(): window = views[col_off][row_off:row_off + rows].reshape(-1, channels)  56.2 us
    slice x10, local copies, waits for them, and re-layouts, back_convolve(): views[2 - col_off][2 - row_off:2 - row_off + rows].reshape(-1, channels)  52.3 us
    unnamed x80, local copies, waits for them, and re-layouts  25 us
    select_n x2, other arithmetic, close_poles(): return jnp.where(keep[:, None, None], padded, jnp.zeros_like(padded))  16.1 us
    all_to_all x1, waiting for transfers between devices, body(): lax.all_to_all(outgoing, ('lat', 'lon'), split_axis=1, concat_axis=1, til...  14.7 us
    dot_general x9, matrix products, back_convolve(): lax.dot_general(window, kernel[row_off, col_off], (((1,), (1,)), ((), ())...  13.6 us
    dot_general x8, matrix products, splat_block(): jnp.dot(spread.astype(jnp.bfloat16), in_features, preferred_element_type=...  12.4 us
  transfers between devices with their start and end apart: 13, of which 6 were waited for; matrix products, arithmetic and copies ran while one was open for 30% of the time, Pallas kernels for 0%

commit v1 on v0

v1 whole, which is shorter than its diff:
```python
import functools
import math

import jax
import jax.numpy as jnp
from jax import lax
from jax.experimental import pallas as pl
from jax.experimental.pallas import tpu as pltpu
from jax.sharding import PartitionSpec as P

BF = jnp.bfloat16
F32 = jnp.float32
MESH = pl.DeviceIdType.MESH
ROWS, COLS, CH, CAP = 32, 128, 256, 16
NLAT, NLON = 8, 16
DEV = NLAT * NLON
SLOTS = DEV * CAP
CELLS = ROWS * COLS
PAIRS = DEV // 2
CHUNKS = 73
EXTRAS = CHUNKS - PAIRS


def iota(shape, dim):
    return lax.broadcasted_iota(jnp.int32, shape, dim)


def fiota(shape, dim):
    return iota(shape, dim).astype(F32)


def aligned(value, unit=128):
    return pl.multiple_of(value, unit)


def remote(src, dst, send, recv, lat, lon):
    return pltpu.make_async_remote_copy(
        src_ref=src, dst_ref=dst, send_sem=send, recv_sem=recv, device_id=(lat, lon), device_id_type=MESH
    )


def wait_bytes(ref, sem):
    pltpu.make_async_copy(ref, ref, sem).wait()


def expand_lanes(meta, onehot, wrf, wrb, dens, edges, edge_inv):
    per_dev = meta[...].reshape(DEV, 128).astype(BF)
    lane = iota((128, 384), 1)
    pick = jnp.where(iota((128, 384), 0) == (lane // 128) * CAP + lane % CAP, 1.0, 0.0).astype(BF)
    spread = jnp.dot(per_dev, pick, preferred_element_type=F32).reshape(16, 8, 384)
    lane8 = iota((8, 384), 1)
    mine = jnp.where(iota((8, 384), 0) == (lane8 % 128) // CAP, 1.0, 0.0)
    flat = (spread * mine[None]).sum(1)
    total = jnp.zeros((2 * ROWS, 128), F32)
    for g in range(16):
        wide = slice(g * 128, g * 128 + 128)
        w, row, col = flat[g : g + 1, 0:128], flat[g : g + 1, 128:256], flat[g : g + 1, 256:384]
        onehot[:, wide] = jnp.where(fiota((COLS, 128), 0) == col, 1.0, 0.0).astype(BF)
        by_row = jnp.where(fiota((ROWS, 128), 0) == row, w, 0.0)
        wrf[:, wide] = by_row
        first = jnp.where(col == 0.0, by_row, 0.0)
        last = jnp.where(col == float(COLS - 1), by_row, 0.0)
        both = jnp.concatenate([first, last], 0)
        edges[:, wide] = both.astype(BF)
        total = total + both
    edge_inv[...] = jnp.broadcast_to(1.0 / (total.sum(1, keepdims=True) + 1.0), (2 * ROWS, 128))

    def widen(r, _):
        wrb[r] = jnp.broadcast_to(wrf[pl.ds(r, 1), :], (16, SLOTS)).astype(BF)
        return 0

    lax.fori_loop(0, ROWS, widen, 0)
    density = lax.dot_general(
        onehot[...], wrf[...].astype(BF), (((1,), (1,)), ((), ())), preferred_element_type=F32
    )
    inv = 1.0 / (density + 1.0)
    for r in range(ROWS):
        dens[r * COLS : (r + 1) * COLS, :] = jnp.broadcast_to(inv[:, r : r + 1], (COLS, 128))


def expand_rows(meta, col_weight, row_of):
    lane = iota((128, 384), 1)
    pick = jnp.where(iota((128, 384), 0) // CAP == lane // 128, 1.0, 0.0).astype(BF)
    slot_lane = iota((CAP, 128), 1)
    mine = jnp.where(slot_lane % CAP == iota((CAP, 128), 0), 1.0, 0.0)

    def step(i, _):
        block = meta[pl.ds(i * 16, 16)]
        masked = (jnp.broadcast_to(block, (16, CAP, 128)) * mine[None]).reshape(256, 128).astype(BF)
        spread = jnp.dot(masked, pick, preferred_element_type=F32)
        base = aligned(i * 256, 256)
        col_weight[pl.ds(base, 256), :] = jnp.where(
            spread[:, 256:384] == fiota((256, 128), 1), spread[:, 0:128], 0.0
        ).astype(BF)
        row_of[pl.ds(base, 256), :] = spread[:, 128:256].astype(BF)
        return 0

    lax.fori_loop(0, DEV // 16, step, 0)


def twice(inv):
    return jnp.concatenate([inv, inv], 1)


def splat_edges(feats, onehot, wrb, dens, edges, edge_inv, rows_out, cols_out):
    hot = onehot[...].reshape(8, 16, SLOTS)
    lhs = jnp.concatenate(
        [(hot * wrb[0][None]).reshape(COLS, SLOTS), (hot * wrb[ROWS - 1][None]).reshape(COLS, SLOTS), edges[...]], 0
    )
    acc = jnp.dot(lhs, feats[...].reshape(SLOTS, CH), preferred_element_type=F32)
    rows_out[0] = (acc[0:COLS] * twice(dens[0:COLS, :])).astype(BF)
    rows_out[1] = (acc[COLS : 2 * COLS] * twice(dens[CELLS - COLS : CELLS, :])).astype(BF)
    cols = (acc[2 * COLS :] * twice(edge_inv[...])).astype(BF)
    cols_out[0] = cols[0:ROWS]
    cols_out[1] = cols[ROWS:]


def splat(feats, onehot, wrb, dens, x3, per=4):
    def step(i, _):
        r0 = i * per
        hot = onehot[...].reshape(8, 16, SLOTS)
        lhs = jnp.concatenate([(hot * wrb[r0 + k][None]).reshape(COLS, SLOTS) for k in range(per)], 0)
        acc = jnp.dot(lhs, feats[...].reshape(SLOTS, CH), preferred_element_type=F32)
        for k in range(per):
            base = aligned((r0 + k) * COLS)
            field = (acc[k * COLS : (k + 1) * COLS] * twice(dens[pl.ds(base, COLS), :])).astype(BF)
            wide = field.astype(F32)
            x3[pl.ds(base + COLS, COLS), 256:512] = field
            x3[pl.ds(base + COLS, COLS), 0:256] = pltpu.roll(wide, 1, 0).astype(BF)
            x3[pl.ds(base + COLS, COLS), 512:768] = pltpu.roll(wide, COLS - 1, 0).astype(BF)
        return 0

    lax.fori_loop(0, ROWS // per, step, 0)


def exchange_edges(lat, lon, rows, cols, h_row, h_col, h_cor, sems):
    up, down = lax.rem(lat + NLAT - 1, NLAT), lax.rem(lat + 1, NLAT)
    west, east = lax.rem(lon + NLON - 1, NLON), lax.rem(lon + 1, NLON)
    plan = (
        (rows[0], h_row.at[1], up, lon),
        (rows[1], h_row.at[0], down, lon),
        (cols.at[0], h_col.at[1], lat, west),
        (cols.at[1], h_col.at[0], lat, east),
        (cols.at[1, pl.ds(16, 16)], h_cor.at[0], down, east),
        (cols.at[0, pl.ds(16, 16)], h_cor.at[1], down, west),
        (cols.at[1, pl.ds(0, 16)], h_cor.at[2], up, east),
        (cols.at[0, pl.ds(0, 16)], h_cor.at[3], up, west),
    )
    return [remote(s, d, sems.at[0, i], sems.at[1, i], a, b) for i, (s, d, a, b) in enumerate(plan)]


def patch(arr, lat, h_row, h_col, h_cor, col_vals, left, right):
    top = jnp.where(lat == 0, 0.0, 1.0)
    bottom = jnp.where(lat == NLAT - 1, 0.0, 1.0)
    for side in range(2):
        col_vals[side, 0:32, :] = h_col[side].astype(F32)
        col_vals[side, 32:40, :] = jnp.broadcast_to(h_cor[side].astype(F32)[15:16] * top, (8, CH))
        col_vals[side, 40:48, :] = jnp.broadcast_to(h_cor[2 + side].astype(F32)[0:1] * bottom, (8, CH))
    sub = iota((16, CH), 0)

    def step(r, _):
        base = aligned((r + 1) * COLS)
        old = arr[pl.ds(base, 16), left : left + CH].astype(F32)
        arr[pl.ds(base, 16), left : left + CH] = jnp.where(sub == 0, col_vals[0, pl.ds(r, 1), :], old).astype(BF)
        far = aligned(base + COLS - 16, 16)
        old = arr[pl.ds(far, 16), right : right + CH].astype(F32)
        arr[pl.ds(far, 16), right : right + CH] = jnp.where(sub == 15, col_vals[1, pl.ds(r, 1), :], old).astype(BF)
        return 0

    lax.fori_loop(0, ROWS, step, 0)
    full = iota((COLS, CH), 0)
    for side, (base, keep) in enumerate(((0, top), ((ROWS + 1) * COLS, bottom))):
        at = 32 + 8 * side
        wide = h_row[side].astype(F32) * keep
        arr[base : base + COLS, 256:512] = wide.astype(BF)
        arr[base : base + COLS, left : left + CH] = jnp.where(
            full == 0, col_vals[0, at : at + 1, :], pltpu.roll(wide, 1, 0)
        ).astype(BF)
        arr[base : base + COLS, right : right + CH] = jnp.where(
            full == COLS - 1, col_vals[1, at : at + 1, :], pltpu.roll(wide, COLS - 1, 0)
        ).astype(BF)


def conv(x3, kc, bias, cot, enc, g3, gsum, gcol, per=4):
    gsum[...] = jnp.zeros_like(gsum)

    def step(i, _):
        r0 = i * per
        acc = jnp.broadcast_to(bias[...], (per * COLS, CH))
        for a in range(3):
            acc = acc + jnp.dot(
                x3[pl.ds(aligned((r0 + a) * COLS), per * COLS), :], kc[a], preferred_element_type=F32
            )
        base = aligned(r0 * COLS)
        gate = 0.5 * jnp.tanh(0.5 * acc) + 0.5
        silu = acc * gate
        field = x3[pl.ds(base + COLS, per * COLS), 256:512].astype(F32)
        enc[pl.ds(base, per * COLS), :] = (field + silu).astype(BF)
        grad = (cot[pl.ds(base, per * COLS), :].astype(F32) * (gate + silu * (1.0 - gate))).astype(BF)
        wide = grad.astype(F32)
        gsum[...] += wide.reshape(per * COLS // 8, 8, CH).sum(0)
        g3[pl.ds(base + COLS, per * COLS), 256:512] = grad
        for k in range(per):
            row = wide[k * COLS : (k + 1) * COLS]
            at = pl.ds(base + COLS + k * COLS, COLS)
            g3[at, 0:256] = pltpu.roll(row, COLS - 1, 0).astype(BF)
            g3[at, 512:768] = pltpu.roll(row, 1, 0).astype(BF)
            gcol[0, pl.ds(r0 + k, 1), :] = row[0:1]
            gcol[1, pl.ds(r0 + k, 1), :] = row[COLS - 1 : COLS]
        return 0

    lax.fori_loop(0, ROWS // per, step, 0)


def back_conv(g3, kt, cot, dens, scaled, per=4):
    def step(i, _):
        r0 = i * per
        base = aligned(r0 * COLS)
        acc = cot[pl.ds(base, per * COLS), :].astype(F32)
        for a in range(3):
            acc = acc + jnp.dot(
                g3[pl.ds(aligned((r0 + 2 - a) * COLS), per * COLS), :], kt[a], preferred_element_type=F32
            )
        scaled[pl.ds(base, per * COLS), :] = (acc * twice(dens[pl.ds(base, per * COLS), :])).astype(BF)
        return 0

    lax.fori_loop(0, ROWS // per, step, 0)


def kernel(
    feat_in, meta_in, kern_in, bias, cot_in,
    enc_out, sums_out, ret_out,
    feats, meta, kc, kt, cot, enc, onehot, wrf, wrb, dens, edges, edge_inv, col_weight, row_of,
    edge_rows, edge_cols, h_row, h_col, h_cor, col_vals, x3, g3, gsum, gcol, grad_cols, scaled, slot_grad,
    dw, pair_dw, pair_sum, half, rs, rs_extra, reduced,
    load_sems, a2a_sems, halo_sems, grad_halo_sems, pair_sems, rs_sems, ag_sems, swap_sems, ret_sems,
):
    lat, lon = lax.axis_index("lat"), lax.axis_index("lon")
    me = lat * NLON + lon
    core = lax.rem(lon, 2)
    mate = lon + 1 - 2 * core
    owner = lat * (NLON // 2) + lon // 2

    def send_meta(j, _):
        to = lax.rem(me + j, DEV)
        remote(meta_in.at[to], meta.at[me], a2a_sems.at[0], a2a_sems.at[1], to // NLON, lax.rem(to, NLON)).start()
        return 0

    def send_feats(j, _):
        to = lax.rem(me + j, DEV)
        remote(feat_in.at[to], feats.at[me], a2a_sems.at[2], a2a_sems.at[3], to // NLON, lax.rem(to, NLON)).start()
        return 0

    own_meta = pltpu.make_async_copy(meta_in.at[me], meta.at[me], load_sems.at[0])
    own_feats = pltpu.make_async_copy(feat_in.at[me], feats.at[me], load_sems.at[1])
    load_kern = pltpu.make_async_copy(kern_in, kc, load_sems.at[2])
    load_cot = pltpu.make_async_copy(cot_in, cot, load_sems.at[3])
    own_meta.start()
    lax.fori_loop(1, DEV, send_meta, 0)
    lax.fori_loop(1, DEV, send_feats, 0)
    own_feats.start()
    load_kern.start()
    load_cot.start()

    load_kern.wait()
    for a in range(3):
        for b in range(3):
            kt[a, b * CH : (b + 1) * CH, :] = kc[a, b * CH : (b + 1) * CH, :].T

    own_meta.wait()
    wait_bytes(meta.at[pl.ds(0, DEV - 1)], a2a_sems.at[1])
    expand_lanes(meta, onehot, wrf, wrb, dens, edges, edge_inv)
    expand_rows(meta, col_weight, row_of)

    own_feats.wait()
    wait_bytes(feats.at[pl.ds(0, DEV - 1)], a2a_sems.at[3])
    splat_edges(feats, onehot, wrb, dens, edges, edge_inv, edge_rows, edge_cols)
    halo = exchange_edges(
        lat, lon, (edge_rows.at[0], edge_rows.at[1]), edge_cols, h_row.at[0], h_col.at[0], h_cor.at[0], halo_sems
    )
    for copy in halo:
        copy.start()
    splat(feats, onehot, wrb, dens, x3)
    for copy in halo:
        copy.wait_recv()
    patch(x3, lat, h_row.at[0], h_col.at[0], h_cor.at[0], col_vals, 0, 512)

    load_cot.wait()
    conv(x3, kc, bias, cot, enc, g3, gsum, gcol)
    store_enc = pltpu.make_async_copy(enc, enc_out, load_sems.at[4])
    store_enc.start()
    grad_cols[...] = gcol[...].astype(BF)
    last = ROWS * COLS
    grad_halo = exchange_edges(
        lat, lon, (g3.at[pl.ds(COLS, COLS), pl.ds(CH, CH)], g3.at[pl.ds(last, COLS), pl.ds(CH, CH)]),
        grad_cols, h_row.at[1], h_col.at[1], h_cor.at[1], grad_halo_sems,
    )
    for copy in grad_halo:
        copy.start()

    pair = []
    for tap in range(9):
        a, b = tap // 3, tap % 3
        dw[tap * CH : (tap + 1) * CH, :] = lax.dot_general(
            x3[a * COLS : a * COLS + CELLS, b * CH : (b + 1) * CH], g3[COLS : COLS + CELLS, CH : 2 * CH],
            (((0,), (0,)), ((), ())), preferred_element_type=F32,
        )
        pair.append(
            remote(
                dw.at[pl.ds(aligned(tap * CH + 128 * (1 - core)), 128)], pair_dw.at[pl.ds(tap * 128, 128)],
                pair_sems.at[0, tap], pair_sems.at[1, tap], lat, mate,
            )
        )
        pair[-1].start()
    pair.append(remote(gsum, pair_sum, pair_sems.at[0, 9], pair_sems.at[1, 9], lat, mate))
    pair[-1].start()

    for copy in grad_halo:
        copy.wait()
    patch(g3, lat, h_row.at[1], h_col.at[1], h_cor.at[1], col_vals, 512, 0)

    for tap in range(9):
        pair[tap].wait()
        mine = dw[pl.ds(aligned(tap * CH + 128 * core), 128), :] + pair_dw[tap * 128 : (tap + 1) * 128, :]
        half[tap * 8 : (tap + 1) * 8] = mine.astype(BF).reshape(8, 16, CH)
    pair[9].wait()
    bias_row = (gsum[...] + pair_sum[...]).sum(0, keepdims=True)
    half[CHUNKS - 1] = jnp.where(iota((16, CH), 0) == 0, bias_row, 0.0).astype(BF)

    def send_chunk(j, _):
        to = lax.rem(owner + j, PAIRS)
        remote(
            half.at[to], rs.at[owner], rs_sems.at[0], rs_sems.at[1], to // 8, lax.rem(to, 8) * 2 + core
        ).start()
        return 0

    lax.fori_loop(1, PAIRS, send_chunk, 0)
    rs[owner] = half[owner]
    for e in range(EXTRAS):
        to = (9 * e) % PAIRS

        @pl.when(owner != to)
        def _():
            remote(
                half.at[PAIRS + e], rs_extra.at[owner], rs_sems.at[2], rs_sems.at[3], to // 8, (to % 8) * 2 + core
            ).start()

        @pl.when(owner == to)
        def _():
            rs_extra[owner] = half[PAIRS + e]

    back_conv(g3, kt, cot, dens, scaled)

    def send_sum(src, dst, send, recv):
        def step(j, _):
            to = lax.rem(owner + j, PAIRS)
            remote(src, dst, send, recv, to // 8, lax.rem(to, 8) * 2 + core).start()
            return 0

        lax.fori_loop(1, PAIRS, step, 0)

    wait_bytes(rs.at[pl.ds(0, PAIRS - 1)], rs_sems.at[1])
    reduced[0] = rs[...].astype(F32).sum(0).astype(BF)
    send_sum(reduced.at[0], sums_out.at[core, owner], ag_sems.at[0], ag_sems.at[1])
    own_sum = pltpu.make_async_copy(reduced.at[0], sums_out.at[core, owner], load_sems.at[5])
    own_sum.start()
    for e in range(EXTRAS):

        @pl.when(owner == (9 * e) % PAIRS)
        def _():
            wait_bytes(rs_extra.at[pl.ds(0, PAIRS - 1)], rs_sems.at[3])
            reduced[1] = rs_extra[...].astype(F32).sum(0).astype(BF)
            spot = sums_out.at[core, PAIRS + e]
            send_sum(reduced.at[1], spot, ag_sems.at[2], ag_sems.at[1])
            own_extra = pltpu.make_async_copy(reduced.at[1], spot, load_sems.at[6])
            own_extra.start()
            own_extra.wait()

    def band(i, _):
        to_lat = lax.rem(lat + i, NLAT)
        base = aligned(to_lat * 256, 256)
        weight, row = col_weight[pl.ds(base, 256), :], row_of[pl.ds(base, 256), :]
        lhs = jnp.concatenate(
            [jnp.where(row == jnp.array(r, BF), weight, jnp.zeros_like(weight)) for r in range(ROWS)], 1
        )
        grads = jnp.dot(lhs, scaled[...], preferred_element_type=F32).astype(BF)
        slot_grad[pl.ds(to_lat * NLON, NLON)] = grads.reshape(NLON, CAP, CH)

        def back(j, _):
            to_lon = lax.rem(lon + j, NLON)
            block = slot_grad.at[to_lat * NLON + to_lon]

            @pl.when(jnp.logical_or(i != 0, j != 0))
            def _():
                remote(block, ret_out.at[me], ret_sems.at[0], ret_sems.at[1], to_lat, to_lon).start()

            return 0

        lax.fori_loop(0, NLON, back, 0)
        return 0

    lax.fori_loop(0, NLAT, band, 0)
    own_ret = pltpu.make_async_copy(slot_grad.at[me], ret_out.at[me], load_sems.at[7])
    own_ret.start()

    own_sum.wait()
    has_extra = functools.reduce(jnp.logical_or, [owner == (9 * e) % PAIRS for e in range(EXTRAS)])

    @pl.when(has_extra)
    def _():
        wait_bytes(sums_out.at[core, pl.ds(0, CHUNKS - 2)], ag_sems.at[1])

    @pl.when(jnp.logical_not(has_extra))
    def _():
        wait_bytes(sums_out.at[core, pl.ds(0, CHUNKS - 1)], ag_sems.at[1])

    swap = remote(sums_out.at[core], sums_out.at[core], swap_sems.at[0], swap_sems.at[1], lat, mate)
    swap.start()

    wait_bytes(ret_out.at[pl.ds(0, DEV - 1)], ret_sems.at[1])
    wait_bytes(slot_grad.at[pl.ds(0, DEV - 1)], ret_sems.at[0])
    wait_bytes(meta.at[pl.ds(0, DEV - 1)], a2a_sems.at[0])
    wait_bytes(feats.at[pl.ds(0, DEV - 1)], a2a_sems.at[2])
    for copy in halo:
        copy.wait_send()
    wait_bytes(rs.at[pl.ds(0, PAIRS - 1)], rs_sems.at[0])
    wait_bytes(rs.at[pl.ds(0, PAIRS - 1)], ag_sems.at[0])

    @pl.when(has_extra)
    def _():
        wait_bytes(rs.at[pl.ds(0, PAIRS - 1)], ag_sems.at[2])
        wait_bytes(half.at[pl.ds(0, EXTRAS - 1)], rs_sems.at[2])

    @pl.when(jnp.logical_not(has_extra))
    def _():
        wait_bytes(half.at[pl.ds(0, EXTRAS)], rs_sems.at[2])

    own_ret.wait()
    store_enc.wait()
    swap.wait()


def fused(feat, meta, kern, bias, cot):
    vm = pltpu.VMEM
    dma = pltpu.SemaphoreType.DMA
    scratch = [
        vm((DEV, CAP, CH), BF),
        vm((DEV, 1, 128), F32),
        vm((3, 3 * CH, CH), BF),
        vm((3, 3 * CH, CH), BF),
        vm((CELLS, CH), BF),
        vm((CELLS, CH), BF),
        vm((COLS, SLOTS), BF),
        vm((ROWS, SLOTS), F32),
        vm((ROWS, 16, SLOTS), BF),
        vm((CELLS, 128), F32),
        vm((2 * ROWS, SLOTS), BF),
        vm((2 * ROWS, 128), F32),
        vm((SLOTS, 128), BF),
        vm((SLOTS, 128), BF),
        vm((2, COLS, CH), BF),
        vm((2, ROWS, CH), BF),
        vm((2, 2, COLS, CH), BF),
        vm((2, 2, ROWS, CH), BF),
        vm((2, 4, 16, CH), BF),
        vm((2, 48, CH), F32),
        vm(((ROWS + 2) * COLS, 3 * CH), BF),
        vm(((ROWS + 2) * COLS, 3 * CH), BF),
        vm((8, CH), F32),
        vm((2, ROWS, CH), F32),
        vm((2, ROWS, CH), BF),
        vm((CELLS, CH), BF),
        vm((DEV, CAP, CH), BF),
        vm((9 * CH, CH), F32),
        vm((9 * 128, CH), F32),
        vm((8, CH), F32),
        vm((CHUNKS, 16, CH), BF),
        vm((PAIRS, 16, CH), BF),
        vm((PAIRS, 16, CH), BF),
        vm((2, 16, CH), BF),
        dma((8,)),
        dma((4,)),
        dma((2, 8)),
        dma((2, 8)),
        dma((2, 10)),
        dma((4,)),
        dma((3,)),
        dma((2,)),
        dma((2,)),
    ]
    anywhere = pl.BlockSpec(memory_space=pl.ANY)
    return pl.pallas_call(
        kernel,
        out_shape=[
            jax.ShapeDtypeStruct((CELLS, CH), BF),
            jax.ShapeDtypeStruct((2, CHUNKS, 16, CH), BF),
            jax.ShapeDtypeStruct((DEV, CAP, CH), BF),
        ],
        in_specs=[anywhere, anywhere, anywhere, pl.BlockSpec(memory_space=pltpu.VMEM), anywhere],
        out_specs=[anywhere] * 3,
        scratch_shapes=scratch,
        compiler_params=pltpu.CompilerParams(has_side_effects=True, vmem_limit_bytes=60 * 2**20),
        name="fused",
    )(feat, meta, kern, bias, cot)


def body(features, offsets, counts, cell_index, kern, conv_bias, cotangent):
    live = jnp.arange(CAP, dtype=jnp.int32)[:, None] < counts[0][None, :]
    radius = offsets[0, 0] * offsets[0, 0] + offsets[1, 0] * offsets[1, 0]
    weights = jnp.where(live, jnp.exp(-2.0 * radius), 0.0)
    row = (cell_index[0] // COLS).astype(F32)
    col = (cell_index[0] % COLS).astype(F32)
    meta = jnp.concatenate([weights, row, col, jnp.zeros((128 - 3 * CAP, DEV), F32)], 0).T.reshape(DEV, 1, 128)
    feat = jnp.transpose(features[0], (1, 0, 2))
    encoded, sums, ret = fused(
        feat, meta, kern.reshape(3, 3 * CH, CH), conv_bias.reshape(1, CH), cotangent.reshape(CELLS, CH)
    )
    scale = 1.0 / math.sqrt(CELLS * DEV)
    taps = sums[:, : CHUNKS - 1].reshape(2, 3, 3, 128, CH).transpose(1, 2, 0, 3, 4).reshape(3, 3, CH, CH)
    weight_grad = taps.astype(F32) * scale
    bias_grad = sums[0, CHUNKS - 1, 0].astype(F32) * scale
    obs_grad = jnp.transpose(ret, (1, 0, 2))[None]
    return encoded.reshape(ROWS, COLS, CH), weight_grad, bias_grad, obs_grad


def solution(mesh):
    return jax.shard_map(
        body,
        mesh=mesh,
        in_specs=(
            P(("lat", "lon"), None, None, None),
            P(None, ("lat", "lon"), None, None),
            P(("lat", "lon"), None),
            P(("lat", "lon"), None, None),
            P(),
            P(),
            P("lat", "lon", None),
        ),
        out_specs=(P("lat", "lon", None), P(), P(), P(("lat", "lon"), None, None, None)),
        check_vma=False,
    )
```

time: 459 us -> 123 us (0.27); the launches traced: 450 us -> 121 us
  local copies, waits for them, and re-layouts: 197 us -> 10.2 us
  Pallas kernels: 0 us -> 107 us
  blocking collectives: 68.2 us -> 0 us
  other arithmetic: 51.6 us -> 3.15 us
  matrix products: 45.3 us -> 0 us
  starting transfers between devices: 38.2 us -> 0 us
  waiting for transfers between devices: 34.4 us -> 0 us
  between operations: 15.1 us -> 0.69 us
    slice x28 -> x1, local copies, waits for them, and re-layouts: 123 us -> 0.1 us  [body(): radius = offsets[0, 0] * offsets[0, 0] + offsets[1, 0] * offsets[1, 0]]
    pallas_call x0 -> x1, Pallas kernels: none -> 107 us  [fused(): pl.pallas_call(kernel, out_shape=[jax.ShapeDtypeStruct((CELLS, CH), BF),...]
    psum x1 -> x0, blocking collectives: 68.2 us -> none  [body(): weight_sum, bias_sum = lax.psum((local_weight, local_bias), ('lat', 'lon'))]
    dot_general x35 -> x0, matrix products: 45.3 us -> none  [the longest x9 13.6 us: back_convolve(): lax.dot_general(window, kernel[row_off, col_off], (((1,), (1,)), ((), ())...]
    all_to_all x4 -> x0, waiting for transfers between devices: 29.9 us -> none  [the longest x1 14.7 us: body(): lax.all_to_all(outgoing, ('lat', 'lon'), split_axis=1, concat_axis=1, til...]
    all_to_all x4 -> x0, starting transfers between devices: 24.5 us -> none  [the longest x1 11.5 us: body(): lax.all_to_all(weights, ('lat', 'lon'), split_axis=1, concat_axis=1, tile...]
    reshape x4 -> x0, local copies, waits for them, and re-layouts: 22.8 us -> none  [the longest x2 11.3 us: body(): gathered = gathered.reshape(cell_total, channels)]
    unnamed x80 -> x8, local copies, waits for them, and re-layouts: 25 us -> 8.4 us
  transfers between devices with their start and end apart: 13 -> 0, of which waited for: 6 -> 0; matrix products, arithmetic and copies ran while one was open for 30% -> 0% of each run, Pallas kernels for 0% -> 0%
where the time goes in v1:
time: 123 us; the launch traced here: 121 us
  Pallas kernels  107 us (87%)
  local copies, waits for them, and re-layouts  10.2 us (8%)
  other arithmetic  3.15 us (3%)
    pallas_call x1, Pallas kernels, fused(): pl.pallas_call(kernel, out_shape=[jax.ShapeDtypeStruct((CELLS, CH), BF),...  107 us
    unnamed x8, local copies, waits for them, and re-layouts  8.4 us

profile of v1, /device:TPU:1, one launch (start us, length us, event | category | flops | bytes accessed | tf_op | source)
XLA Modules:
  0.0 121.5 jit_solution(640986632336126617)
XLA Ops:
  0.6 0.1 pad.3.clone
  0.7 0.7 fusion.5
  1.4 0.1 copy.20
  1.5 0.1 copy.22
  1.6 0.7 bitcast_select_fusion
  2.4 0.8 copy.23
  3.2 0.1 fusion
  3.2 0.7 maximum_maximum_fusion
  4.0 2.8 %copy.27 = bf16[1,16,128,256]{3,1,2,0:T(8,128)(2,1)} copy(bf16[1,16,128,256]{3,2,1,0:T(8,128)(2,1)} %param.7) | data formatting | bytes 2097152 | tf_op args[0]
  6.8 107.4 %fused.1 = (bf16[4096,256]{1,0:T(8,128)(2,1)}, bf16[2,73,16,256]{3,2,1,0:T(8,128)(2,1)}, bf16[128,16,256]{2,1,0:T(8,128)(2,1)}) custom-call(bf16[128,16,256]{2,1,0:T(8,128)(2,1)} %bitcast.50, f32[128,1,128]{2,1,0:T(1,128)} %bitcast.56, bf16[3,768,256]{2,1,0:T(8,128)(2,1)} %bitcast.54, f32[1,256]{1,0:T(1,128)} %bitcast.57, bf16[4096,256]{1,0:T(8,128)(2,1)} %bitcast.52), custom_call_target="tpu_custom_call" | custom-call | tf_op jit(solution)/shard_map/fused/pallas_call | solution.py:492
  114.1 0.0 copy-start.1
  114.2 2.6 %copy.25 = bf16[1,16,128,256]{3,2,1,0:T(8,128)(2,1)} copy(bf16[1,16,128,256]{3,1,2,0:T(8,128)(2,1)} %bitcast.55) | data formatting | bytes 2097152
  116.8 0.0 copy-done.1
  116.8 0.6 convert_multiply_fusion.1
  117.4 0.3 convert_multiply_fusion
  117.7 0.0 copy-start
  117.7 1.6 %copy.24 = f32[3,3,2,128,256]{4,3,2,1,0:T(8,128)} copy(f32[3,3,2,128,256]{4,3,1,0,2:T(8,128)S(1)} %bitcast.49) | data formatting | bytes 4718592 | tf_op jit(solution)/shard_map/mul | solution.py:520
  119.3 0.9 copy-done
  120.1 1.3 %copy.29 = bf16[32,128,256]{2,1,0:T(8,128)(2,1)} copy(bf16[32,128,256]{2,1,0:T(8,128)(2,1)S(1)} %bitcast.53) | data formatting | bytes 4194304
  (1 shorter events, 0.0 us)
Async XLA Ops:
  114.1 2.6 %copy-start.1 = (bf16[2,73,16,256]{3,2,1,0:T(8,128)(2,1)S(1)}, bf16[2,73,16,256]{3,2,1,0:T(8,128)(2,1)}, u32[]{:S(2)}) copy-start(bf16[2,73,16,256]{3,2,1,0:T(8,128)(2,1)} %get-tuple-element.8) | copy-start | bytes 3588100
  117.7 2.4 %copy-start = (bf16[4096,256]{1,0:T(8,128)(2,1)S(1)}, bf16[4096,256]{1,0:T(8,128)(2,1)}, u32[]{:S(2)}) copy-start(bf16[4096,256]{1,0:T(8,128)(2,1)} %get-tuple-element.7) | copy-start | bytes 6291460

commit v2 on v1

--- a/solution.py
+++ b/solution.py
@@ -17,8 +17,8 @@
 SLOTS = DEV * CAP
 CELLS = ROWS * COLS
 PAIRS = DEV // 2
-CHUNKS = 73
-EXTRAS = CHUNKS - PAIRS
+CHIPS = NLON // 2
+CHUNKS = 72
 
 
 def iota(shape, dim):
@@ -212,6 +212,30 @@
     lax.fori_loop(0, ROWS // per, step, 0)
 
 
+def wgrad_tap(tap, x3, g3, dw):
+    a, b = tap // 3, tap % 3
+    dw[tap * CH : (tap + 1) * CH, :] = lax.dot_general(
+        x3[a * COLS : a * COLS + CELLS, b * CH : (b + 1) * CH], g3[COLS : COLS + CELLS, CH : 2 * CH],
+        (((0,), (0,)), ((), ())), preferred_element_type=F32,
+    )
+
+
+def grad_band(i, col_weight, row_of, scaled, slot_grad):
+    base = aligned(i * 256, 256)
+    weight, row = col_weight[pl.ds(base, 256), :], row_of[pl.ds(base, 256), :]
+    lhs = jnp.concatenate(
+        [jnp.where(row == jnp.array(r, BF), weight, jnp.zeros_like(weight)) for r in range(ROWS)], 1
+    )
+    grads = jnp.dot(lhs, scaled[...], preferred_element_type=F32).astype(BF)
+    slot_grad[pl.ds(i * 16, 16)] = grads.reshape(16, CAP, CH)
+
+
+def transpose_kernel(kc, kt):
+    for a in range(3):
+        for b in range(3):
+            kt[a, b * CH : (b + 1) * CH, :] = kc[a, b * CH : (b + 1) * CH, :].T
+
+
 def back_conv(g3, kt, cot, dens, scaled, per=4):
     def step(i, _):
         r0 = i * per
@@ -227,53 +251,141 @@
     lax.fori_loop(0, ROWS // per, step, 0)
 
 
+def place(p):
+    q = lax.rem(p, 16)
+    a = q // 2
+    return a, lax.rem(2 * (p // 16 + a) + lax.rem(q, 2), NLON)
+
+
+def spread_over(j):
+    b = lax.rem(j, CHIPS)
+    return lax.rem(j // CHIPS + b, NLAT), b
+
+
+def first_chunk(lat, chip):
+    rank = lax.rem(chip - lat + CHIPS, CHIPS)
+    return rank, 9 * lat + rank + jnp.where(rank > 0, 1, 0)
+
+
+def slot_meta(offsets, counts, cells, turned, meta_src):
+    live = iota((CAP, DEV), 0) < counts[...]
+    radius = offsets[0] * offsets[0] + offsets[1] * offsets[1]
+    weight = jnp.where(live, jnp.exp(-2.0 * radius), 0.0)
+    row, col = cells[...] // COLS, cells[...] % COLS
+    table = jnp.concatenate([weight, row.astype(F32), col.astype(F32), jnp.zeros((128 - 3 * CAP, DEV), F32)], 0)
+    turned[...] = table.T
+
+    def step(t, _):
+        meta_src[lax.rem(t, NLON), t // NLON] = turned[pl.ds(t, 1), :]
+        return 0
+
+    lax.fori_loop(0, DEV, step, 0, unroll=8)
+
+
+def turn_slots(by_slot, wide, by_dest):
+    flat = by_slot[...].reshape(SLOTS, CH).astype(F32)
+    wide[0], wide[1] = flat[:, :128], flat[:, 128:]
+
+    def step(t, _):
+        halves = [wide[h, pl.ds(t, CAP, stride=DEV), :] for h in range(2)]
+        by_dest[t] = jnp.concatenate(halves, 1).astype(BF)
+        return 0
+
+    lax.fori_loop(0, DEV, step, 0, unroll=8)
+
+
 def kernel(
-    feat_in, meta_in, kern_in, bias, cot_in,
-    enc_out, sums_out, ret_out,
+    feat_in, offsets, counts, cells, kern_in, bias, cot_in,
+    enc_out, sums_out, ret_out, bias_out,
+    by_slot, wide, by_dest, turned, meta_src, meta_mid, meta_nat,
     feats, meta, kc, kt, cot, enc, onehot, wrf, wrb, dens, edges, edge_inv, col_weight, row_of,
     edge_rows, edge_cols, h_row, h_col, h_cor, col_vals, x3, g3, gsum, gcol, grad_cols, scaled, slot_grad,
-    dw, pair_dw, pair_sum, half, rs, rs_extra, reduced,
-    load_sems, a2a_sems, halo_sems, grad_halo_sems, pair_sems, rs_sems, ag_sems, swap_sems, ret_sems,
+    dw, pair_dw, pair_sum, half, rs, reduced, bias_lat, bias_mid, bias_lon,
+    round_sem, load_sems, a2a_sems, halo_sems, grad_halo_sems, pair_sems, rs_sems, ag_sems, swap_sems, ret_sems, bias_sems,
 ):
     lat, lon = lax.axis_index("lat"), lax.axis_index("lon")
     me = lat * NLON + lon
     core = lax.rem(lon, 2)
     mate = lon + 1 - 2 * core
-    owner = lat * (NLON // 2) + lon // 2
-
-    def send_meta(j, _):
-        to = lax.rem(me + j, DEV)
-        remote(meta_in.at[to], meta.at[me], a2a_sems.at[0], a2a_sems.at[1], to // NLON, lax.rem(to, NLON)).start()
-        return 0
-
-    def send_feats(j, _):
-        to = lax.rem(me + j, DEV)
-        remote(feat_in.at[to], feats.at[me], a2a_sems.at[2], a2a_sems.at[3], to // NLON, lax.rem(to, NLON)).start()
-        return 0
-
-    own_meta = pltpu.make_async_copy(meta_in.at[me], meta.at[me], load_sems.at[0])
-    own_feats = pltpu.make_async_copy(feat_in.at[me], feats.at[me], load_sems.at[1])
+    chip = lon // 2
+    owner = lat * CHIPS + chip
+    rank, mine = first_chunk(lat, chip)
+
+    def over_lat(j):
+        return lax.rem(lat + j, NLAT)
+
+    def over_lon(j):
+        return lax.rem(lon + j, NLON)
+
+    load_feat = pltpu.make_async_copy(feat_in, by_slot, load_sems.at[1])
     load_kern = pltpu.make_async_copy(kern_in, kc, load_sems.at[2])
     load_cot = pltpu.make_async_copy(cot_in, cot, load_sems.at[3])
-    own_meta.start()
-    lax.fori_loop(1, DEV, send_meta, 0)
-    lax.fori_loop(1, DEV, send_feats, 0)
-    own_feats.start()
+    load_feat.start()
     load_kern.start()
     load_cot.start()
 
+    barrier = pltpu.get_barrier_semaphore()
+
+    def greet_lon(j, _):
+        pl.semaphore_signal(barrier, inc=1, device_id=(lat, over_lon(j)), device_id_type=MESH)
+        return 0
+
+    def greet_lat(j, _):
+        pl.semaphore_signal(barrier, inc=1, device_id=(over_lat(j), lon), device_id_type=MESH)
+        return 0
+
+    def vouch(j, _):
+        pl.semaphore_signal(round_sem, inc=1, device_id=(over_lat(j), lon), device_id_type=MESH)
+        return 0
+
+    lax.fori_loop(1, NLON, greet_lon, 0)
+    lax.fori_loop(1, NLAT, greet_lat, 0)
+    slot_meta(offsets, counts, cells, turned, meta_src)
+    load_feat.wait()
+    turn_slots(by_slot, wide, by_dest)
+    pl.semaphore_wait(barrier, NLON + NLAT - 2)
+    lax.fori_loop(1, NLAT, vouch, 0)
+
+    def meta_lon(j, _):
+        to = over_lon(j)
+        remote(meta_src.at[to], meta_mid.at[lon], a2a_sems.at[0], a2a_sems.at[1], lat, to).start()
+        return 0
+
+    def meta_lat(j, _):
+        to = over_lat(j)
+        remote(meta_mid.at[pl.ds(0, NLON), to], meta_nat.at[lat], a2a_sems.at[2], a2a_sems.at[3], to, lon).start()
+        return 0
+
+    def send_feats(p, _):
+        a, b = place(p)
+        to_lat, to_lon = lax.rem(lat - a + NLAT, NLAT), lax.rem(lon - b + NLON, NLON)
+        remote(by_dest.at[to_lat * NLON + to_lon], feats.at[p], a2a_sems.at[4], a2a_sems.at[5], to_lat, to_lon).start()
+        return 0
+
+    lax.fori_loop(1, NLON, meta_lon, 0)
+    meta_mid[lon] = meta_src[lon]
+    pl.semaphore_wait(round_sem, NLAT - 1)
+    lax.fori_loop(1, DEV // 2, send_feats, 0)
+    wait_bytes(meta_mid.at[pl.ds(0, NLON - 1)], a2a_sems.at[1])
+    lax.fori_loop(1, NLAT, meta_lat, 0)
+    meta_nat[lat] = meta_mid[:, lat]
+    lax.fori_loop(DEV // 2, DEV, send_feats, 0)
+    feats[0] = by_dest[me]
+
     load_kern.wait()
-    for a in range(3):
-        for b in range(3):
-            kt[a, b * CH : (b + 1) * CH, :] = kc[a, b * CH : (b + 1) * CH, :].T
-
-    own_meta.wait()
-    wait_bytes(meta.at[pl.ds(0, DEV - 1)], a2a_sems.at[1])
+    transpose_kernel(kc, kt)
+    wait_bytes(meta_nat.at[pl.ds(0, NLAT - 1)], a2a_sems.at[3])
+
+    def reorder(p, _):
+        a, b = place(p)
+        meta[p] = meta_nat[over_lat(a), over_lon(b)]
+        return 0
+
+    lax.fori_loop(0, DEV, reorder, 0, unroll=4)
     expand_lanes(meta, onehot, wrf, wrb, dens, edges, edge_inv)
     expand_rows(meta, col_weight, row_of)
 
-    own_feats.wait()
-    wait_bytes(feats.at[pl.ds(0, DEV - 1)], a2a_sems.at[3])
+    wait_bytes(feats.at[pl.ds(0, DEV - 1)], a2a_sems.at[5])
     splat_edges(feats, onehot, wrb, dens, edges, edge_inv, edge_rows, edge_cols)
     halo = exchange_edges(
         lat, lon, (edge_rows.at[0], edge_rows.at[1]), edge_cols, h_row.at[0], h_col.at[0], h_cor.at[0], halo_sems
@@ -298,13 +410,10 @@
     for copy in grad_halo:
         copy.start()
 
-    pair = []
+    pair = [remote(gsum, pair_sum, pair_sems.at[0, 9], pair_sems.at[1, 9], lat, mate)]
+    pair[0].start()
     for tap in range(9):
-        a, b = tap // 3, tap % 3
-        dw[tap * CH : (tap + 1) * CH, :] = lax.dot_general(
-            x3[a * COLS : a * COLS + CELLS, b * CH : (b + 1) * CH], g3[COLS : COLS + CELLS, CH : 2 * CH],
-            (((0,), (0,)), ((), ())), preferred_element_type=F32,
-        )
+        wgrad_tap(tap, x3, g3, dw)
         pair.append(
             remote(
                 dw.at[pl.ds(aligned(tap * CH + 128 * (1 - core)), 128)], pair_dw.at[pl.ds(tap * 128, 128)],
@@ -312,138 +421,157 @@
             )
         )
         pair[-1].start()
-    pair.append(remote(gsum, pair_sum, pair_sems.at[0, 9], pair_sems.at[1, 9], lat, mate))
-    pair[-1].start()
 
     for copy in grad_halo:
         copy.wait()
     patch(g3, lat, h_row.at[1], h_col.at[1], h_cor.at[1], col_vals, 512, 0)
 
+    pair[0].wait()
+    bias_lat[lat] = gsum[...] + pair_sum[...]
     for tap in range(9):
-        pair[tap].wait()
-        mine = dw[pl.ds(aligned(tap * CH + 128 * core), 128), :] + pair_dw[tap * 128 : (tap + 1) * 128, :]
-        half[tap * 8 : (tap + 1) * 8] = mine.astype(BF).reshape(8, 16, CH)
-    pair[9].wait()
-    bias_row = (gsum[...] + pair_sum[...]).sum(0, keepdims=True)
-    half[CHUNKS - 1] = jnp.where(iota((16, CH), 0) == 0, bias_row, 0.0).astype(BF)
+        pair[tap + 1].wait()
+        total = dw[pl.ds(aligned(tap * CH + 128 * core), 128), :] + pair_dw[tap * 128 : (tap + 1) * 128, :]
+        half[tap * 8 : (tap + 1) * 8] = total.astype(BF).reshape(8, 16, CH)
 
     def send_chunk(j, _):
-        to = lax.rem(owner + j, PAIRS)
-        remote(
-            half.at[to], rs.at[owner], rs_sems.at[0], rs_sems.at[1], to // 8, lax.rem(to, 8) * 2 + core
-        ).start()
+        a, b = spread_over(j)
+        to_lat, to_chip = over_lat(a), lax.rem(chip + b, CHIPS)
+        to_rank, at = first_chunk(to_lat, to_chip)
+
+        def send(count):
+            remote(
+                half.at[pl.ds(at, count)], rs.at[owner, pl.ds(0, count)], rs_sems.at[0], rs_sems.at[1],
+                to_lat, to_chip * 2 + core,
+            ).start()
+
+        @pl.when(to_rank == 0)
+        def _():
+            send(2)
+
+        @pl.when(to_rank != 0)
+        def _():
+            send(1)
+
+        return 0
+
+    def send_bias_lat(j, _):
+        remote(bias_lat.at[lat], bias_lat.at[lat], bias_sems.at[0], bias_sems.at[1], over_lat(j), lon).start()
         return 0
 
     lax.fori_loop(1, PAIRS, send_chunk, 0)
-    rs[owner] = half[owner]
-    for e in range(EXTRAS):
-        to = (9 * e) % PAIRS
-
-        @pl.when(owner != to)
-        def _():
+    lax.fori_loop(1, NLAT, send_bias_lat, 0)
+    rs[owner, 0] = half[mine]
+
+    @pl.when(rank == 0)
+    def _():
+        rs[owner, 1] = half[mine + 1]
+
+    back_conv(g3, kt, cot, dens, scaled)
+
+    def send_sum(count):
+        spot = sums_out.at[core, pl.ds(mine, count)]
+        own = pltpu.make_async_copy(reduced.at[pl.ds(0, count)], spot, load_sems.at[5])
+        own.start()
+
+        def step(j, _):
+            a, b = spread_over(j)
+            to_chip = lax.rem(chip + b, CHIPS)
             remote(
-                half.at[PAIRS + e], rs_extra.at[owner], rs_sems.at[2], rs_sems.at[3], to // 8, (to % 8) * 2 + core
+                reduced.at[pl.ds(0, count)], spot, ag_sems.at[0], ag_sems.at[1], over_lat(a), to_chip * 2 + core
             ).start()
-
-        @pl.when(owner == to)
-        def _():
-            rs_extra[owner] = half[PAIRS + e]
-
-    back_conv(g3, kt, cot, dens, scaled)
-
-    def send_sum(src, dst, send, recv):
-        def step(j, _):
-            to = lax.rem(owner + j, PAIRS)
-            remote(src, dst, send, recv, to // 8, lax.rem(to, 8) * 2 + core).start()
             return 0
 
         lax.fori_loop(1, PAIRS, step, 0)
 
-    wait_bytes(rs.at[pl.ds(0, PAIRS - 1)], rs_sems.at[1])
-    reduced[0] = rs[...].astype(F32).sum(0).astype(BF)
-    send_sum(reduced.at[0], sums_out.at[core, owner], ag_sems.at[0], ag_sems.at[1])
-    own_sum = pltpu.make_async_copy(reduced.at[0], sums_out.at[core, owner], load_sems.at[5])
-    own_sum.start()
-    for e in range(EXTRAS):
-
-        @pl.when(owner == (9 * e) % PAIRS)
-        def _():
-            wait_bytes(rs_extra.at[pl.ds(0, PAIRS - 1)], rs_sems.at[3])
-            reduced[1] = rs_extra[...].astype(F32).sum(0).astype(BF)
-            spot = sums_out.at[core, PAIRS + e]
-            send_sum(reduced.at[1], spot, ag_sems.at[2], ag_sems.at[1])
-            own_extra = pltpu.make_async_copy(reduced.at[1], spot, load_sems.at[6])
-            own_extra.start()
-            own_extra.wait()
+    @pl.when(rank == 0)
+    def _():
+        wait_bytes(rs.at[pl.ds(0, PAIRS - 1)], rs_sems.at[1])
+        reduced[...] = rs[...].astype(F32).sum(0).astype(BF)
+        send_sum(2)
+
+    @pl.when(rank != 0)
+    def _():
+        wait_bytes(half.at[pl.ds(0, PAIRS - 1)], rs_sems.at[1])
+        reduced[0] = rs[:, 0].astype(F32).sum(0).astype(BF)
+        send_sum(1)
+
+    wait_bytes(bias_lat.at[pl.ds(0, NLAT - 1)], bias_sems.at[1])
+    bias_mid[...] = bias_lat[...].sum(0)
+    bias_lon[chip] = bias_mid[...]
+
+    def send_bias_lon(j, _):
+        to_chip = lax.rem(chip + j, CHIPS)
+        remote(bias_mid, bias_lon.at[chip], bias_sems.at[2], bias_sems.at[3], lat, to_chip * 2 + core).start()
+        return 0
+
+    lax.fori_loop(1, CHIPS, send_bias_lon, 0)
 
     def band(i, _):
-        to_lat = lax.rem(lat + i, NLAT)
-        base = aligned(to_lat * 256, 256)
-        weight, row = col_weight[pl.ds(base, 256), :], row_of[pl.ds(base, 256), :]
-        lhs = jnp.concatenate(
-            [jnp.where(row == jnp.array(r, BF), weight, jnp.zeros_like(weight)) for r in range(ROWS)], 1
-        )
-        grads = jnp.dot(lhs, scaled[...], preferred_element_type=F32).astype(BF)
-        slot_grad[pl.ds(to_lat * NLON, NLON)] = grads.reshape(NLON, CAP, CH)
+        grad_band(i, col_weight, row_of, scaled, slot_grad)
 
         def back(j, _):
-            to_lon = lax.rem(lon + j, NLON)
-            block = slot_grad.at[to_lat * NLON + to_lon]
-
-            @pl.when(jnp.logical_or(i != 0, j != 0))
+            p = i * 16 + j
+            a, b = place(p)
+
+            @pl.when(p != 0)
             def _():
-                remote(block, ret_out.at[me], ret_sems.at[0], ret_sems.at[1], to_lat, to_lon).start()
+                remote(
+                    slot_grad.at[p], ret_out.at[me], ret_sems.at[0], ret_sems.at[1], over_lat(a), over_lon(b)
+                ).start()
 
             return 0
 
-        lax.fori_loop(0, NLON, back, 0)
-        return 0
-
-    lax.fori_loop(0, NLAT, band, 0)
-    own_ret = pltpu.make_async_copy(slot_grad.at[me], ret_out.at[me], load_sems.at[7])
+        lax.fori_loop(0, 16, back, 0)
+        return 0
+
+    lax.fori_loop(0, DEV // 16, band, 0)
+    own_ret = pltpu.make_async_copy(slot_grad.at[0], ret_out.at[me], load_sems.at[7])
     own_ret.start()
 
-    own_sum.wait()
-    has_extra = functools.reduce(jnp.logical_or, [owner == (9 * e) % PAIRS for e in range(EXTRAS)])
-
-    @pl.when(has_extra)
+    @pl.when(rank == 0)
     def _():
+        pltpu.make_async_copy(reduced, sums_out.at[core, pl.ds(mine, 2)], load_sems.at[5]).wait()
         wait_bytes(sums_out.at[core, pl.ds(0, CHUNKS - 2)], ag_sems.at[1])
-
-    @pl.when(jnp.logical_not(has_extra))
+        wait_bytes(rs.at[pl.ds(0, PAIRS - 1)], ag_sems.at[0])
+        wait_bytes(half.at[pl.ds(0, CHUNKS - 2)], rs_sems.at[0])
+
+    @pl.when(rank != 0)
     def _():
+        pltpu.make_async_copy(reduced.at[pl.ds(0, 1)], sums_out.at[core, pl.ds(mine, 1)], load_sems.at[5]).wait()
         wait_bytes(sums_out.at[core, pl.ds(0, CHUNKS - 1)], ag_sems.at[1])
+        wait_bytes(half.at[pl.ds(0, PAIRS - 1)], ag_sems.at[0])
+        wait_bytes(half.at[pl.ds(0, CHUNKS - 1)], rs_sems.at[0])
 
     swap = remote(sums_out.at[core], sums_out.at[core], swap_sems.at[0], swap_sems.at[1], lat, mate)
     swap.start()
-
-    wait_bytes(ret_out.at[pl.ds(0, DEV - 1)], ret_sems.at[1])
-    wait_bytes(slot_grad.at[pl.ds(0, DEV - 1)], ret_sems.at[0])
-    wait_bytes(meta.at[pl.ds(0, DEV - 1)], a2a_sems.at[0])
-    wait_bytes(feats.at[pl.ds(0, DEV - 1)], a2a_sems.at[2])
+    wait_bytes(bias_lon.at[pl.ds(0, CHIPS - 1)], bias_sems.at[3])
+    bias_out[...] = bias_lon[...].sum(0).sum(0, keepdims=True)
+
+    wait_bytes(meta_mid.at[pl.ds(0, NLON - 1)], a2a_sems.at[0])
+    wait_bytes(meta_nat.at[pl.ds(0, NLAT - 1)], a2a_sems.at[2])
+    wait_bytes(feats.at[pl.ds(0, DEV - 1)], a2a_sems.at[4])
+    wait_bytes(bias_lat.at[pl.ds(0, NLAT - 1)], bias_sems.at[0])
+    wait_bytes(bias_lon.at[pl.ds(0, CHIPS - 1)], bias_sems.at[2])
     for copy in halo:
         copy.wait_send()
-    wait_bytes(rs.at[pl.ds(0, PAIRS - 1)], rs_sems.at[0])
-    wait_bytes(rs.at[pl.ds(0, PAIRS - 1)], ag_sems.at[0])
-
-    @pl.when(has_extra)
-    def _():
-        wait_bytes(rs.at[pl.ds(0, PAIRS - 1)], ag_sems.at[2])
-        wait_bytes(half.at[pl.ds(0, EXTRAS - 1)], rs_sems.at[2])
-
-    @pl.when(jnp.logical_not(has_extra))
-    def _():
-        wait_bytes(half.at[pl.ds(0, EXTRAS)], rs_sems.at[2])
-
+    store_enc.wait()
     own_ret.wait()
-    store_enc.wait()
+    wait_bytes(slot_grad.at[pl.ds(0, DEV - 1)], ret_sems.at[0])
+    wait_bytes(ret_out.at[pl.ds(0, DEV - 1)], ret_sems.at[1])
     swap.wait()
 
 
-def fused(feat, meta, kern, bias, cot):
+def fused(feat, offsets, counts, cells, kern, bias, cot):
     vm = pltpu.VMEM
     dma = pltpu.SemaphoreType.DMA
     scratch = [
+        vm((CAP, DEV, CH), BF),
+        vm((2, SLOTS, 128), F32),
+        vm((DEV, CAP, CH), BF),
+        vm((DEV, 128), F32),
+        vm((NLON, NLAT, 1, 128), F32),
+        vm((NLON, NLAT, 1, 128), F32),
+        vm((NLAT, NLON, 1, 128), F32),
         vm((DEV, CAP, CH), BF),
         vm((DEV, 1, 128), F32),
         vm((3, 3 * CH, CH), BF),
@@ -475,50 +603,50 @@
         vm((9 * 128, CH), F32),
         vm((8, CH), F32),
         vm((CHUNKS, 16, CH), BF),
-        vm((PAIRS, 16, CH), BF),
-        vm((PAIRS, 16, CH), BF),
+        vm((PAIRS, 2, 16, CH), BF),
         vm((2, 16, CH), BF),
+        vm((NLAT, 8, CH), F32),
+        vm((8, CH), F32),
+        vm((CHIPS, 8, CH), F32),
+        pltpu.SemaphoreType.REGULAR,
         dma((8,)),
-        dma((4,)),
+        dma((6,)),
         dma((2, 8)),
         dma((2, 8)),
         dma((2, 10)),
-        dma((4,)),
-        dma((3,)),
         dma((2,)),
         dma((2,)),
+        dma((2,)),
+        dma((2,)),
+        dma((4,)),
     ]
     anywhere = pl.BlockSpec(memory_space=pl.ANY)
+    local = pl.BlockSpec(memory_space=pltpu.VMEM)
     return pl.pallas_call(
         kernel,
         out_shape=[
             jax.ShapeDtypeStruct((CELLS, CH), BF),
             jax.ShapeDtypeStruct((2, CHUNKS, 16, CH), BF),
             jax.ShapeDtypeStruct((DEV, CAP, CH), BF),
+            jax.ShapeDtypeStruct((1, CH), F32),
         ],
-        in_specs=[anywhere, anywhere, anywhere, pl.BlockSpec(memory_space=pltpu.VMEM), anywhere],
-        out_specs=[anywhere] * 3,
+        in_specs=[anywhere, local, local, local, anywhere, local, anywhere],
+        out_specs=[anywhere, anywhere, anywhere, local],
         scratch_shapes=scratch,
-        compiler_params=pltpu.CompilerParams(has_side_effects=True, vmem_limit_bytes=60 * 2**20),
+        compiler_params=pltpu.CompilerParams(collective_id=0, has_side_effects=True, vmem_limit_bytes=60 * 2**20),
         name="fused",
-    )(feat, meta, kern, bias, cot)
+    )(feat, offsets, counts, cells, kern, bias, cot)
 
 
 def body(features, offsets, counts, cell_index, kern, conv_bias, cotangent):
-    live = jnp.arange(CAP, dtype=jnp.int32)[:, None] < counts[0][None, :]
-    radius = offsets[0, 0] * offsets[0, 0] + offsets[1, 0] * offsets[1, 0]
-    weights = jnp.where(live, jnp.exp(-2.0 * radius), 0.0)
-    row = (cell_index[0] // COLS).astype(F32)
-    col = (cell_index[0] % COLS).astype(F32)
-    meta = jnp.concatenate([weights, row, col, jnp.zeros((128 - 3 * CAP, DEV), F32)], 0).T.reshape(DEV, 1, 128)
-    feat = jnp.transpose(features[0], (1, 0, 2))
-    encoded, sums, ret = fused(
-        feat, meta, kern.reshape(3, 3 * CH, CH), conv_bias.reshape(1, CH), cotangent.reshape(CELLS, CH)
+    encoded, sums, ret, bias_sum = fused(
+        features[0], offsets[:, 0], counts, cell_index[0], kern.reshape(3, 3 * CH, CH),
+        conv_bias.reshape(1, CH), cotangent.reshape(CELLS, CH),
     )
     scale = 1.0 / math.sqrt(CELLS * DEV)
-    taps = sums[:, : CHUNKS - 1].reshape(2, 3, 3, 128, CH).transpose(1, 2, 0, 3, 4).reshape(3, 3, CH, CH)
+    taps = sums.reshape(2, 3, 3, 128, CH).transpose(1, 2, 0, 3, 4).reshape(3, 3, CH, CH)
     weight_grad = taps.astype(F32) * scale
-    bias_grad = sums[0, CHUNKS - 1, 0].astype(F32) * scale
+    bias_grad = bias_sum[0] * scale
     obs_grad = jnp.transpose(ret, (1, 0, 2))[None]
     return encoded.reshape(ROWS, COLS, CH), weight_grad, bias_grad, obs_grad
 

time: 123 us -> 112 us (0.911)
  the two profiles are of different devices: /device:TPU:1 before, /device:TPU:0 now
where the time goes in v2:
time: 112 us; the launch traced here: 111 us
  Pallas kernels  103 us (92%)
  local copies, waits for them, and re-layouts  6.29 us (6%)
  other arithmetic  1.64 us (1%)
    pallas_call x1, Pallas kernels, fused(): pl.pallas_call(kernel, out_shape=[jax.ShapeDtypeStruct((CELLS, CH), BF),...  103 us
    unnamed x6, local copies, waits for them, and re-layouts  4.73 us

profile of v2, /device:TPU:0, one launch (start us, length us, event | category | flops | bytes accessed | tf_op | source)
XLA Modules:
  0.0 111.5 jit_solution(13767749896280883740)
XLA Ops:
  0.6 102.9 %fused.1 = (bf16[4096,256]{1,0:T(8,128)(2,1)}, bf16[2,72,16,256]{3,2,1,0:T(8,128)(2,1)}, bf16[128,16,256]{2,1,0:T(8,128)(2,1)}, f32[1,256]{1,0:T(1,128)}) custom-call(bf16[16,128,256]{2,1,0:T(8,128)(2,1)} %bitcast.20, f32[2,16,128]{2,1,0:T(8,128)} %bitcast.22, s32[1,128]{1,0:T(1,128)} %counts.1, s32[16,128]{1,0:T(8,128)} %bitcast.23, ...), custom_call_target="tpu_custom_call" | custom-call | tf_op jit(solution)/shard_map/fused/pallas_call | solution.py:625
  103.5 0.0 copy-start.1
  103.5 1.3 %broadcast_multiply_fusion = f32[1,256]{1,0:T(1,128)} fusion(f32[1,256]{1,0:T(1,128)} %get-tuple-element.10), kind=kLoop, calls=%fused_computation.1 | loop fusion | flops 256 | bytes 2048 | tf_op jit(solution)/shard_map/mul | solution.py:649
  104.8 2.5 %copy.12 = bf16[1,16,128,256]{3,2,1,0:T(8,128)(2,1)} copy(bf16[1,16,128,256]{3,1,2,0:T(8,128)(2,1)} %bitcast.21) | data formatting | bytes 2097152
  107.4 0.0 copy-done.1
  107.4 0.3 convert_multiply_fusion
  107.7 0.0 copy-start
  107.7 1.6 %copy.11 = f32[3,3,2,128,256]{4,3,2,1,0:T(8,128)} copy(f32[3,3,2,128,256]{4,3,1,0,2:T(8,128)S(1)} %bitcast.15) | data formatting | bytes 4718592 | tf_op jit(solution)/shard_map/mul | solution.py:648
  109.3 0.9 copy-done
  110.1 1.3 %copy.14 = bf16[32,128,256]{2,1,0:T(8,128)(2,1)} copy(bf16[32,128,256]{2,1,0:T(8,128)(2,1)S(1)} %bitcast.18) | data formatting | bytes 4194304
Async XLA Ops:
  103.5 3.9 %copy-start.1 = (bf16[2,72,16,256]{3,2,1,0:T(8,128)(2,1)S(1)}, bf16[2,72,16,256]{3,2,1,0:T(8,128)(2,1)}, u32[]{:S(2)}) copy-start(bf16[2,72,16,256]{3,2,1,0:T(8,128)(2,1)} %get-tuple-element.9) | copy-start | bytes 3538948
  107.7 2.4 %copy-start = (bf16[4096,256]{1,0:T(8,128)(2,1)S(1)}, bf16[4096,256]{1,0:T(8,128)(2,1)}, u32[]{:S(2)}) copy-start(bf16[4096,256]{1,0:T(8,128)(2,1)} %get-tuple-element.8) | copy-start | bytes 6291460

commit v3 on v2

--- a/solution.py
+++ b/solution.py
@@ -19,6 +19,8 @@
 PAIRS = DEV // 2
 CHIPS = NLON // 2
 CHUNKS = 72
+TAPS = 9
+LAG = 2
 
 
 def iota(shape, dim):
@@ -212,11 +214,10 @@
     lax.fori_loop(0, ROWS // per, step, 0)
 
 
-def wgrad_tap(tap, x3, g3, dw):
-    a, b = tap // 3, tap % 3
-    dw[tap * CH : (tap + 1) * CH, :] = lax.dot_general(
-        x3[a * COLS : a * COLS + CELLS, b * CH : (b + 1) * CH], g3[COLS : COLS + CELLS, CH : 2 * CH],
-        (((0,), (0,)), ((), ())), preferred_element_type=F32,
+def wgrad_tap(step, tap, x3, g3, dw):
+    rows, lanes = pl.ds(aligned(tap // 3 * COLS), CELLS), pl.ds(aligned(lax.rem(tap, 3) * CH), CH)
+    dw[step] = lax.dot_general(
+        x3[rows, lanes], g3[COLS : COLS + CELLS, CH : 2 * CH], (((0,), (0,)), ((), ())), preferred_element_type=F32
     )
 
 
@@ -262,11 +263,6 @@
     return lax.rem(j // CHIPS + b, NLAT), b
 
 
-def first_chunk(lat, chip):
-    rank = lax.rem(chip - lat + CHIPS, CHIPS)
-    return rank, 9 * lat + rank + jnp.where(rank > 0, 1, 0)
-
-
 def slot_meta(offsets, counts, cells, turned, meta_src):
     live = iota((CAP, DEV), 0) < counts[...]
     radius = offsets[0] * offsets[0] + offsets[1] * offsets[1]
@@ -300,8 +296,8 @@
     by_slot, wide, by_dest, turned, meta_src, meta_mid, meta_nat,
     feats, meta, kc, kt, cot, enc, onehot, wrf, wrb, dens, edges, edge_inv, col_weight, row_of,
     edge_rows, edge_cols, h_row, h_col, h_cor, col_vals, x3, g3, gsum, gcol, grad_cols, scaled, slot_grad,
-    dw, pair_dw, pair_sum, half, rs, reduced, bias_lat, bias_mid, bias_lon,
-    round_sem, load_sems, a2a_sems, halo_sems, grad_halo_sems, pair_sems, rs_sems, ag_sems, swap_sems, ret_sems, bias_sems,
+    dw, pair_dw, pair_sum, half, rs, reduced, bias_lat, bias_mid, bias_lon, tail_chip, tail_lat, tail_part, tail_sum,
+    round_sem, load_sems, a2a_sems, halo_sems, grad_halo_sems, pair_sems, rs_sems, ag_sems, swap_sems, ret_sems, bias_sems, tail_sems,
 ):
     lat, lon = lax.axis_index("lat"), lax.axis_index("lon")
     me = lat * NLON + lon
@@ -309,7 +305,7 @@
     mate = lon + 1 - 2 * core
     chip = lon // 2
     owner = lat * CHIPS + chip
-    rank, mine = first_chunk(lat, chip)
+    mine = lax.rem(lat - chip + CHIPS, CHIPS) * CHIPS + chip
 
     def over_lat(j):
         return lax.rem(lat + j, NLAT)
@@ -410,101 +406,134 @@
     for copy in grad_halo:
         copy.start()
 
-    pair = [remote(gsum, pair_sum, pair_sems.at[0, 9], pair_sems.at[1, 9], lat, mate)]
-    pair[0].start()
-    for tap in range(9):
-        wgrad_tap(tap, x3, g3, dw)
+    pair_bias = remote(gsum, pair_sum, pair_sems.at[0, TAPS], pair_sems.at[1, TAPS], lat, mate)
+    pair_bias.start()
+    taps = [jnp.int32(8)] + [lax.rem(lat + chip + i, 8) for i in range(8)]
+    pair = []
+
+    def pair_total(step):
+        pair[step].wait()
+        total = dw[step, pl.ds(aligned(128 * core), 128), :] + pair_dw[step]
+        half[step] = total.astype(BF).reshape(8, 16, CH)
+
+    def last_tap_rows(_):
+        pair_total(0)
+        tail_chip[chip] = half[0, chip]
+
+        def step(j, _):
+            to = lax.rem(chip + j, CHIPS)
+            remote(half.at[0, to], tail_chip.at[chip], tail_sems.at[0], tail_sems.at[1], lat, to * 2 + core).start()
+            return 0
+
+        lax.fori_loop(1, CHIPS, step, 0)
+
+    def last_tap_columns(_):
+        wait_bytes(tail_chip.at[pl.ds(0, CHIPS - 1)], tail_sems.at[1])
+        tail_part[...] = tail_chip[...].astype(F32).sum(0).astype(BF)
+        tail_lat[lat] = tail_part[...]
+
+        def step(j, _):
+            remote(tail_part, tail_lat.at[lat], tail_sems.at[2], tail_sems.at[3], over_lat(j), lon).start()
+            return 0
+
+        lax.fori_loop(1, NLAT, step, 0)
+
+    def last_tap_gather(_):
+        wait_bytes(tail_lat.at[pl.ds(0, NLAT - 1)], tail_sems.at[3])
+        tail_sum[...] = tail_lat[...].astype(F32).sum(0).astype(BF)
+        spot = sums_out.at[core, PAIRS + chip]
+        pltpu.make_async_copy(tail_sum, spot, load_sems.at[6]).start()
+
+        def step(j, _):
+            to = lax.rem(chip + j, CHIPS)
+            remote(tail_sum, spot, tail_sems.at[4], tail_sems.at[5], lat, to * 2 + core).start()
+            return 0
+
+        lax.fori_loop(1, CHIPS, step, 0)
+
+    def bias_columns(_):
+        pair_bias.wait()
+        bias_lat[lat] = gsum[...] + pair_sum[...]
+
+        def step(j, _):
+            remote(bias_lat.at[lat], bias_lat.at[lat], bias_sems.at[0], bias_sems.at[1], over_lat(j), lon).start()
+            return 0
+
+        lax.fori_loop(1, NLAT, step, 0)
+
+    def bias_rows(_):
+        wait_bytes(bias_lat.at[pl.ds(0, NLAT - 1)], bias_sems.at[1])
+        bias_mid[...] = bias_lat[...].sum(0)
+        bias_lon[chip] = bias_mid[...]
+
+        def step(j, _):
+            to = lax.rem(chip + j, CHIPS)
+            remote(bias_mid, bias_lon.at[chip], bias_sems.at[2], bias_sems.at[3], lat, to * 2 + core).start()
+            return 0
+
+        lax.fori_loop(1, CHIPS, step, 0)
+
+    def send_tap(step):
+        pair_total(step)
+        tap = taps[step]
+
+        def send(m, _):
+            to_lat = lax.rem(tap + m, NLAT)
+            here = jnp.logical_and(to_lat == lat, m == chip)
+
+            @pl.when(jnp.logical_not(here))
+            def _():
+                remote(
+                    half.at[step, m], rs.at[owner], rs_sems.at[0], rs_sems.at[1], to_lat, m * 2 + core
+                ).start()
+
+            @pl.when(here)
+            def _():
+                rs[owner] = half[step, m]
+
+            return 0
+
+        lax.fori_loop(0, CHIPS, send, 0)
+
+    def send_pair(step):
         pair.append(
             remote(
-                dw.at[pl.ds(aligned(tap * CH + 128 * (1 - core)), 128)], pair_dw.at[pl.ds(tap * 128, 128)],
-                pair_sems.at[0, tap], pair_sems.at[1, tap], lat, mate,
+                dw.at[step, pl.ds(aligned(128 * (1 - core)), 128)], pair_dw.at[step],
+                pair_sems.at[0, step], pair_sems.at[1, step], lat, mate,
             )
         )
         pair[-1].start()
 
+    beside = {1: bias_columns, 2: last_tap_rows, 4: bias_rows, 5: last_tap_columns, 8: last_tap_gather}
+    for step in range(TAPS):
+        wgrad_tap(step, taps[step], x3, g3, dw)
+        send_pair(step)
+        if step in beside:
+            beside[step](step)
+        if step > LAG:
+            send_tap(step - LAG)
+
     for copy in grad_halo:
         copy.wait()
     patch(g3, lat, h_row.at[1], h_col.at[1], h_cor.at[1], col_vals, 512, 0)
-
-    pair[0].wait()
-    bias_lat[lat] = gsum[...] + pair_sum[...]
-    for tap in range(9):
-        pair[tap + 1].wait()
-        total = dw[pl.ds(aligned(tap * CH + 128 * core), 128), :] + pair_dw[tap * 128 : (tap + 1) * 128, :]
-        half[tap * 8 : (tap + 1) * 8] = total.astype(BF).reshape(8, 16, CH)
-
-    def send_chunk(j, _):
+    for step in range(TAPS - LAG, TAPS):
+        send_tap(step)
+
+    wait_bytes(rs.at[pl.ds(0, PAIRS - 1)], rs_sems.at[1])
+    reduced[...] = rs[...].astype(F32).sum(0).astype(BF)
+    own_sum = pltpu.make_async_copy(reduced, sums_out.at[core, mine], load_sems.at[5])
+    own_sum.start()
+
+    def send_sum(j, _):
         a, b = spread_over(j)
-        to_lat, to_chip = over_lat(a), lax.rem(chip + b, CHIPS)
-        to_rank, at = first_chunk(to_lat, to_chip)
-
-        def send(count):
-            remote(
-                half.at[pl.ds(at, count)], rs.at[owner, pl.ds(0, count)], rs_sems.at[0], rs_sems.at[1],
-                to_lat, to_chip * 2 + core,
-            ).start()
-
-        @pl.when(to_rank == 0)
-        def _():
-            send(2)
-
-        @pl.when(to_rank != 0)
-        def _():
-            send(1)
-
-        return 0
-
-    def send_bias_lat(j, _):
-        remote(bias_lat.at[lat], bias_lat.at[lat], bias_sems.at[0], bias_sems.at[1], over_lat(j), lon).start()
-        return 0
-
-    lax.fori_loop(1, PAIRS, send_chunk, 0)
-    lax.fori_loop(1, NLAT, send_bias_lat, 0)
-    rs[owner, 0] = half[mine]
-
-    @pl.when(rank == 0)
-    def _():
-        rs[owner, 1] = half[mine + 1]
-
+        to_chip = lax.rem(chip + b, CHIPS)
+        remote(
+            reduced, sums_out.at[core, mine], ag_sems.at[0], ag_sems.at[1], over_lat(a), to_chip * 2 + core
+        ).start()
+        return 0
+
+    lax.fori_loop(1, PAIRS, send_sum, 0)
     back_conv(g3, kt, cot, dens, scaled)
-
-    def send_sum(count):
-        spot = sums_out.at[core, pl.ds(mine, count)]
-        own = pltpu.make_async_copy(reduced.at[pl.ds(0, count)], spot, load_sems.at[5])
-        own.start()
-
-        def step(j, _):
-            a, b = spread_over(j)
-            to_chip = lax.rem(chip + b, CHIPS)
-            remote(
-                reduced.at[pl.ds(0, count)], spot, ag_sems.at[0], ag_sems.at[1], over_lat(a), to_chip * 2 + core
-            ).start()
-            return 0
-
-        lax.fori_loop(1, PAIRS, step, 0)
-
-    @pl.when(rank == 0)
-    def _():
-        wait_bytes(rs.at[pl.ds(0, PAIRS - 1)], rs_sems.at[1])
-        reduced[...] = rs[...].astype(F32).sum(0).astype(BF)
-        send_sum(2)
-
-    @pl.when(rank != 0)
-    def _():
-        wait_bytes(half.at[pl.ds(0, PAIRS - 1)], rs_sems.at[1])
-        reduced[0] = rs[:, 0].astype(F32).sum(0).astype(BF)
-        send_sum(1)
-
-    wait_bytes(bias_lat.at[pl.ds(0, NLAT - 1)], bias_sems.at[1])
-    bias_mid[...] = bias_lat[...].sum(0)
-    bias_lon[chip] = bias_mid[...]
-
-    def send_bias_lon(j, _):
-        to_chip = lax.rem(chip + j, CHIPS)
-        remote(bias_mid, bias_lon.at[chip], bias_sems.at[2], bias_sems.at[3], lat, to_chip * 2 + core).start()
-        return 0
-
-    lax.fori_loop(1, CHIPS, send_bias_lon, 0)
 
     def band(i, _):
         grad_band(i, col_weight, row_of, scaled, slot_grad)
@@ -528,20 +557,10 @@
     own_ret = pltpu.make_async_copy(slot_grad.at[0], ret_out.at[me], load_sems.at[7])
     own_ret.start()
 
-    @pl.when(rank == 0)
-    def _():
-        pltpu.make_async_copy(reduced, sums_out.at[core, pl.ds(mine, 2)], load_sems.at[5]).wait()
-        wait_bytes(sums_out.at[core, pl.ds(0, CHUNKS - 2)], ag_sems.at[1])
-        wait_bytes(rs.at[pl.ds(0, PAIRS - 1)], ag_sems.at[0])
-        wait_bytes(half.at[pl.ds(0, CHUNKS - 2)], rs_sems.at[0])
-
-    @pl.when(rank != 0)
-    def _():
-        pltpu.make_async_copy(reduced.at[pl.ds(0, 1)], sums_out.at[core, pl.ds(mine, 1)], load_sems.at[5]).wait()
-        wait_bytes(sums_out.at[core, pl.ds(0, CHUNKS - 1)], ag_sems.at[1])
-        wait_bytes(half.at[pl.ds(0, PAIRS - 1)], ag_sems.at[0])
-        wait_bytes(half.at[pl.ds(0, CHUNKS - 1)], rs_sems.at[0])
-
+    own_sum.wait()
+    pltpu.make_async_copy(tail_sum, sums_out.at[core, PAIRS + chip], load_sems.at[6]).wait()
+    wait_bytes(sums_out.at[core, pl.ds(0, PAIRS - 1)], ag_sems.at[1])
+    wait_bytes(sums_out.at[core, pl.ds(0, CHIPS - 1)], tail_sems.at[5])
     swap = remote(sums_out.at[core], sums_out.at[core], swap_sems.at[0], swap_sems.at[1], lat, mate)
     swap.start()
     wait_bytes(bias_lon.at[pl.ds(0, CHIPS - 1)], bias_sems.at[3])
@@ -552,6 +571,11 @@
     wait_bytes(feats.at[pl.ds(0, DEV - 1)], a2a_sems.at[4])
     wait_bytes(bias_lat.at[pl.ds(0, NLAT - 1)], bias_sems.at[0])
     wait_bytes(bias_lon.at[pl.ds(0, CHIPS - 1)], bias_sems.at[2])
+    wait_bytes(tail_chip.at[pl.ds(0, CHIPS - 1)], tail_sems.at[0])
+    wait_bytes(tail_lat.at[pl.ds(0, NLAT - 1)], tail_sems.at[2])
+    wait_bytes(tail_chip.at[pl.ds(0, CHIPS - 1)], tail_sems.at[4])
+    wait_bytes(rs.at[pl.ds(0, PAIRS - 1)], rs_sems.at[0])
+    wait_bytes(rs.at[pl.ds(0, PAIRS - 1)], ag_sems.at[0])
     for copy in halo:
         copy.wait_send()
     store_enc.wait()
@@ -599,15 +623,19 @@
         vm((2, ROWS, CH), BF),
         vm((CELLS, CH), BF),
         vm((DEV, CAP, CH), BF),
-        vm((9 * CH, CH), F32),
-        vm((9 * 128, CH), F32),
+        vm((TAPS, CH, CH), F32),
+        vm((TAPS, 128, CH), F32),
         vm((8, CH), F32),
-        vm((CHUNKS, 16, CH), BF),
-        vm((PAIRS, 2, 16, CH), BF),
-        vm((2, 16, CH), BF),
+        vm((TAPS, CHIPS, 16, CH), BF),
+        vm((PAIRS, 16, CH), BF),
+        vm((16, CH), BF),
         vm((NLAT, 8, CH), F32),
         vm((8, CH), F32),
         vm((CHIPS, 8, CH), F32),
+        vm((CHIPS, 16, CH), BF),
+        vm((NLAT, 16, CH), BF),
+        vm((16, CH), BF),
+        vm((16, CH), BF),
         pltpu.SemaphoreType.REGULAR,
         dma((8,)),
         dma((6,)),
@@ -619,6 +647,7 @@
         dma((2,)),
         dma((2,)),
         dma((4,)),
+        dma((6,)),
     ]
     anywhere = pl.BlockSpec(memory_space=pl.ANY)
     local = pl.BlockSpec(memory_space=pltpu.VMEM)

time: 112 us -> 101 us (0.902)
  the two profiles are of different devices: /device:TPU:0 before, /device:TPU:1 now
where the time goes in v3:
time: 101 us; the launch traced here: 100 us
  Pallas kernels  91.7 us (91%)
  local copies, waits for them, and re-layouts  6.29 us (6%)
  other arithmetic  1.64 us (2%)
    pallas_call x1, Pallas kernels, fused(): pl.pallas_call(kernel, out_shape=[jax.ShapeDtypeStruct((CELLS, CH), BF),...  91.7 us
    unnamed x6, local copies, waits for them, and re-layouts  4.73 us

profile of v3, /device:TPU:1, one launch (start us, length us, event | category | flops | bytes accessed | tf_op | source)
XLA Modules:
  0.0 100.3 jit_solution(11818071899549302052)
XLA Ops:
  0.6 91.7 %fused.1 = (bf16[4096,256]{1,0:T(8,128)(2,1)}, bf16[2,72,16,256]{3,2,1,0:T(8,128)(2,1)}, bf16[128,16,256]{2,1,0:T(8,128)(2,1)}, f32[1,256]{1,0:T(1,128)}) custom-call(bf16[16,128,256]{2,1,0:T(8,128)(2,1)} %bitcast.20, f32[2,16,128]{2,1,0:T(8,128)} %bitcast.22, s32[1,128]{1,0:T(1,128)} %counts.1, s32[16,128]{1,0:T(8,128)} %bitcast.23, ...), custom_call_target="tpu_custom_call" | custom-call | tf_op jit(solution)/shard_map/fused/pallas_call | solution.py:654
  92.4 0.0 copy-start.1
  92.4 1.3 %broadcast_multiply_fusion = f32[1,256]{1,0:T(1,128)} fusion(f32[1,256]{1,0:T(1,128)} %get-tuple-element.10), kind=kLoop, calls=%fused_computation.1 | loop fusion | flops 256 | bytes 2048 | tf_op jit(solution)/shard_map/mul | solution.py:678
  93.7 2.5 %copy.12 = bf16[1,16,128,256]{3,2,1,0:T(8,128)(2,1)} copy(bf16[1,16,128,256]{3,1,2,0:T(8,128)(2,1)} %bitcast.21) | data formatting | bytes 2097152
  96.2 0.0 copy-done.1
  96.2 0.3 convert_multiply_fusion
  96.6 0.0 copy-start
  96.6 1.6 %copy.11 = f32[3,3,2,128,256]{4,3,2,1,0:T(8,128)} copy(f32[3,3,2,128,256]{4,3,1,0,2:T(8,128)S(1)} %bitcast.15) | data formatting | bytes 4718592 | tf_op jit(solution)/shard_map/mul | solution.py:677
  98.1 0.9 copy-done
  99.0 1.3 %copy.14 = bf16[32,128,256]{2,1,0:T(8,128)(2,1)} copy(bf16[32,128,256]{2,1,0:T(8,128)(2,1)S(1)} %bitcast.18) | data formatting | bytes 4194304
Async XLA Ops:
  92.4 3.9 %copy-start.1 = (bf16[2,72,16,256]{3,2,1,0:T(8,128)(2,1)S(1)}, bf16[2,72,16,256]{3,2,1,0:T(8,128)(2,1)}, u32[]{:S(2)}) copy-start(bf16[2,72,16,256]{3,2,1,0:T(8,128)(2,1)} %get-tuple-element.9) | copy-start | bytes 3538948
  96.6 2.4 %copy-start = (bf16[4096,256]{1,0:T(8,128)(2,1)S(1)}, bf16[4096,256]{1,0:T(8,128)(2,1)}, u32[]{:S(2)}) copy-start(bf16[4096,256]{1,0:T(8,128)(2,1)} %get-tuple-element.8) | copy-start | bytes 6291460

commit v4 on v3

--- a/solution.py
+++ b/solution.py
@@ -337,8 +337,6 @@
     lax.fori_loop(1, NLON, greet_lon, 0)
     lax.fori_loop(1, NLAT, greet_lat, 0)
     slot_meta(offsets, counts, cells, turned, meta_src)
-    load_feat.wait()
-    turn_slots(by_slot, wide, by_dest)
     pl.semaphore_wait(barrier, NLON + NLAT - 2)
     lax.fori_loop(1, NLAT, vouch, 0)
 
@@ -360,6 +358,8 @@
 
     lax.fori_loop(1, NLON, meta_lon, 0)
     meta_mid[lon] = meta_src[lon]
+    load_feat.wait()
+    turn_slots(by_slot, wide, by_dest)
     pl.semaphore_wait(round_sem, NLAT - 1)
     lax.fori_loop(1, DEV // 2, send_feats, 0)
     wait_bytes(meta_mid.at[pl.ds(0, NLON - 1)], a2a_sems.at[1])
@@ -416,7 +416,7 @@
         total = dw[step, pl.ds(aligned(128 * core), 128), :] + pair_dw[step]
         half[step] = total.astype(BF).reshape(8, 16, CH)
 
-    def last_tap_rows(_):
+    def last_tap_rows():
         pair_total(0)
         tail_chip[chip] = half[0, chip]
 
@@ -427,7 +427,7 @@
 
         lax.fori_loop(1, CHIPS, step, 0)
 
-    def last_tap_columns(_):
+    def last_tap_columns():
         wait_bytes(tail_chip.at[pl.ds(0, CHIPS - 1)], tail_sems.at[1])
         tail_part[...] = tail_chip[...].astype(F32).sum(0).astype(BF)
         tail_lat[lat] = tail_part[...]
@@ -438,7 +438,7 @@
 
         lax.fori_loop(1, NLAT, step, 0)
 
-    def last_tap_gather(_):
+    def last_tap_gather():
         wait_bytes(tail_lat.at[pl.ds(0, NLAT - 1)], tail_sems.at[3])
         tail_sum[...] = tail_lat[...].astype(F32).sum(0).astype(BF)
         spot = sums_out.at[core, PAIRS + chip]
@@ -451,7 +451,7 @@
 
         lax.fori_loop(1, CHIPS, step, 0)
 
-    def bias_columns(_):
+    def bias_columns():
         pair_bias.wait()
         bias_lat[lat] = gsum[...] + pair_sum[...]
 
@@ -461,7 +461,7 @@
 
         lax.fori_loop(1, NLAT, step, 0)
 
-    def bias_rows(_):
+    def bias_rows():
         wait_bytes(bias_lat.at[pl.ds(0, NLAT - 1)], bias_sems.at[1])
         bias_mid[...] = bias_lat[...].sum(0)
         bias_lon[chip] = bias_mid[...]
@@ -504,12 +504,12 @@
         )
         pair[-1].start()
 
-    beside = {1: bias_columns, 2: last_tap_rows, 4: bias_rows, 5: last_tap_columns, 8: last_tap_gather}
+    beside = {3: last_tap_rows, 6: bias_columns}
     for step in range(TAPS):
         wgrad_tap(step, taps[step], x3, g3, dw)
         send_pair(step)
         if step in beside:
-            beside[step](step)
+            beside[step]()
         if step > LAG:
             send_tap(step - LAG)
 
@@ -518,6 +518,10 @@
     patch(g3, lat, h_row.at[1], h_col.at[1], h_cor.at[1], col_vals, 512, 0)
     for step in range(TAPS - LAG, TAPS):
         send_tap(step)
+
+    last_tap_columns()
+    bias_rows()
+    back_conv(g3, kt, cot, dens, scaled)
 
     wait_bytes(rs.at[pl.ds(0, PAIRS - 1)], rs_sems.at[1])
     reduced[...] = rs[...].astype(F32).sum(0).astype(BF)
@@ -533,7 +537,7 @@
         return 0
 
     lax.fori_loop(1, PAIRS, send_sum, 0)
-    back_conv(g3, kt, cot, dens, scaled)
+    last_tap_gather()
 
     def band(i, _):
         grad_band(i, col_weight, row_of, scaled, slot_grad)
@@ -667,17 +671,84 @@
     )(feat, offsets, counts, cells, kern, bias, cot)
 
 
+def finish_kernel(
+    enc_in, sums_in, ret_in, bias_in, enc_out, grad_out, bias_out, obs_out, enc, sums, ret, grad, wide, obs, sems, out_sems
+):
+    scale = 1.0 / math.sqrt(CELLS * DEV)
+    load_ret = pltpu.make_async_copy(ret_in, ret, sems.at[0])
+    load_sums = pltpu.make_async_copy(sums_in, sums, sems.at[1])
+    load_enc = pltpu.make_async_copy(enc_in, enc, sems.at[2])
+    load_sums.start()
+    load_ret.start()
+    load_enc.start()
+    bias_out[...] = bias_in[...] * scale
+    copies = []
+
+    def store(src, dst):
+        copies.append(pltpu.make_async_copy(src, dst, out_sems.at[len(copies)]))
+        copies[-1].start()
+
+    load_sums.wait()
+    for tap in range(TAPS):
+        for core in range(2):
+            rows = sums[core, tap * CHIPS : (tap + 1) * CHIPS].reshape(128, CH)
+            grad[tap, core * 128 : (core + 1) * 128, :] = rows.astype(F32) * scale
+        store(grad.at[tap], grad_out.at[tap])
+    load_enc.wait()
+    store(enc, enc_out)
+    load_ret.wait()
+    flat = ret[...].reshape(SLOTS, CH).astype(F32)
+    wide[0], wide[1] = flat[:, :128], flat[:, 128:]
+    for k in range(CAP):
+        halves = [wide[h, pl.ds(k, DEV, stride=CAP), :] for h in range(2)]
+        obs[k] = jnp.concatenate(halves, 1).astype(BF)
+        if k % 4 == 3:
+            store(obs.at[pl.ds(k - 3, 4)], obs_out.at[pl.ds(k - 3, 4)])
+    for copy in copies:
+        copy.wait()
+
+
+def finish(encoded, sums, ret, bias_sum):
+    vm = pltpu.VMEM
+    anywhere = pl.BlockSpec(memory_space=pl.ANY)
+    local = pl.BlockSpec(memory_space=pltpu.VMEM)
+    return pl.pallas_call(
+        finish_kernel,
+        out_shape=[
+            jax.ShapeDtypeStruct((CELLS, CH), BF),
+            jax.ShapeDtypeStruct((TAPS, CH, CH), F32),
+            jax.ShapeDtypeStruct((1, CH), F32),
+            jax.ShapeDtypeStruct((CAP, DEV, CH), BF),
+        ],
+        in_specs=[anywhere, anywhere, anywhere, local],
+        out_specs=[anywhere, anywhere, local, anywhere],
+        scratch_shapes=[
+            vm((CELLS, CH), BF),
+            vm((2, CHUNKS, 16, CH), BF),
+            vm((DEV, CAP, CH), BF),
+            vm((TAPS, CH, CH), F32),
+            vm((2, SLOTS, 128), F32),
+            vm((CAP, DEV, CH), BF),
+            pltpu.SemaphoreType.DMA((3,)),
+            pltpu.SemaphoreType.DMA((16,)),
+        ],
+        compiler_params=pltpu.CompilerParams(vmem_limit_bytes=56 * 2**20),
+        name="finish",
+    )(encoded, sums, ret, bias_sum)
+
+
 def body(features, offsets, counts, cell_index, kern, conv_bias, cotangent):
     encoded, sums, ret, bias_sum = fused(
         features[0], offsets[:, 0], counts, cell_index[0], kern.reshape(3, 3 * CH, CH),
         conv_bias.reshape(1, CH), cotangent.reshape(CELLS, CH),
     )
-    scale = 1.0 / math.sqrt(CELLS * DEV)
-    taps = sums.reshape(2, 3, 3, 128, CH).transpose(1, 2, 0, 3, 4).reshape(3, 3, CH, CH)
-    weight_grad = taps.astype(F32) * scale
-    bias_grad = bias_sum[0] * scale
-    obs_grad = jnp.transpose(ret, (1, 0, 2))[None]
-    return encoded.reshape(ROWS, COLS, CH), weight_grad, bias_grad, obs_grad
+    encoded, weight_grad, bias_grad, obs_grad = finish(encoded, sums, ret, bias_sum)
+    return (
+        encoded.reshape(ROWS, COLS, CH),
+        weight_grad.reshape(3, 3, CH, CH),
+        bias_grad.reshape(CH),
+        obs_grad[None],
+    )
 
 
 def solution(mesh):

time: 101 us -> 93.8 us (0.929)
  local copies, waits for them, and re-layouts: 6.29 us -> 0 us
  other arithmetic: 1.64 us -> 0 us
  Pallas kernels: 91.7 us -> 93 us
    pallas_call x0 -> x1, Pallas kernels: none -> 5.42 us  [finish(): pl.pallas_call(finish_kernel, out_shape=[jax.ShapeDtypeStruct((CELLS, CH)...]
    unnamed x6 -> x0, local copies, waits for them, and re-layouts: 4.73 us -> none
    pallas_call x1, Pallas kernels: 91.7 us -> 87.5 us  [fused(): pl.pallas_call(kernel, out_shape=[jax.ShapeDtypeStruct((CELLS, CH), BF),...]
    mul x2 -> x0, other arithmetic: 1.64 us -> none  [the longest x1 1.32 us: body(): bias_grad = bias_sum[0] * scale]
    mul x1 -> x0, local copies, waits for them, and re-layouts: 1.56 us -> none  [body(): weight_grad = taps.astype(F32) * scale]
where the time goes in v4:
time: 93.8 us; the launch traced here: 93.6 us
  Pallas kernels  93 us (99%)
    pallas_call x1, Pallas kernels, fused(): pl.pallas_call(kernel, out_shape=[jax.ShapeDtypeStruct((CELLS, CH), BF),...  87.5 us
    pallas_call x1, Pallas kernels, finish(): pl.pallas_call(finish_kernel, out_shape=[jax.ShapeDtypeStruct((CELLS, CH)...  5.42 us

profile of v4, /device:TPU:1, one launch (start us, length us, event | category | flops | bytes accessed | tf_op | source)
XLA Modules:
  0.0 93.6 jit_solution(1264440851184182487)
XLA Ops:
  0.6 87.5 %fused.1 = (bf16[4096,256]{1,0:T(8,128)(2,1)}, bf16[2,72,16,256]{3,2,1,0:T(8,128)(2,1)}, bf16[128,16,256]{2,1,0:T(8,128)(2,1)}, f32[1,256]{1,0:T(1,128)}) custom-call(bf16[16,128,256]{2,1,0:T(8,128)(2,1)} %bitcast.12, f32[2,16,128]{2,1,0:T(8,128)} %bitcast.13, s32[1,128]{1,0:T(1,128)} %counts.1, s32[16,128]{1,0:T(8,128)} %bitcast.14, ...), custom_call_target="tpu_custom_call" | custom-call | tf_op jit(solution)/shard_map/fused/pallas_call | solution.py:658
  88.2 5.4 %finish.1 = (bf16[4096,256]{1,0:T(8,128)(2,1)}, f32[9,256,256]{2,1,0:T(8,128)}, f32[1,256]{1,0:T(1,128)}, bf16[16,128,256]{2,1,0:T(8,128)(2,1)}) custom-call(bf16[4096,256]{1,0:T(8,128)(2,1)} %get-tuple-element.12.enc_in, bf16[2,72,16,256]{3,2,1,0:T(8,128)(2,1)} %get-tuple-element.13.sums_in, bf16[128,16,256]{2,1,0:T(8,128)(2,1)} %get-tuple-element.14.ret_in, ...), custom_call_target="tpu_custom_call" | custom-call | tf_op jit(solution)/shard_map/finish/pallas_call | solution.py:715

commit v5 on v4

--- a/solution.py
+++ b/solution.py
@@ -183,7 +183,7 @@
         ).astype(BF)
 
 
-def conv(x3, kc, bias, cot, enc, g3, gsum, gcol, per=4):
+def conv(x3, kc, bias, cot, enc, g3, gsum, gcol, per=8):
     gsum[...] = jnp.zeros_like(gsum)
 
     def step(i, _):
@@ -237,9 +237,9 @@
             kt[a, b * CH : (b + 1) * CH, :] = kc[a, b * CH : (b + 1) * CH, :].T
 
 
-def back_conv(g3, kt, cot, dens, scaled, per=4):
+def back_conv(first, count, g3, kt, cot, dens, scaled, per=8):
     def step(i, _):
-        r0 = i * per
+        r0 = first + i * per
         base = aligned(r0 * COLS)
         acc = cot[pl.ds(base, per * COLS), :].astype(F32)
         for a in range(3):
@@ -249,7 +249,7 @@
         scaled[pl.ds(base, per * COLS), :] = (acc * twice(dens[pl.ds(base, per * COLS), :])).astype(BF)
         return 0
 
-    lax.fori_loop(0, ROWS // per, step, 0)
+    lax.fori_loop(0, count // per, step, 0)
 
 
 def place(p):
@@ -521,7 +521,7 @@
 
     last_tap_columns()
     bias_rows()
-    back_conv(g3, kt, cot, dens, scaled)
+    back_conv(0, ROWS // 2, g3, kt, cot, dens, scaled)
 
     wait_bytes(rs.at[pl.ds(0, PAIRS - 1)], rs_sems.at[1])
     reduced[...] = rs[...].astype(F32).sum(0).astype(BF)
@@ -537,6 +537,7 @@
         return 0
 
     lax.fori_loop(1, PAIRS, send_sum, 0)
+    back_conv(ROWS // 2, ROWS // 2, g3, kt, cot, dens, scaled)
     last_tap_gather()
 
     def band(i, _):
@@ -557,9 +558,7 @@
         lax.fori_loop(0, 16, back, 0)
         return 0
 
-    lax.fori_loop(0, DEV // 16, band, 0)
-    own_ret = pltpu.make_async_copy(slot_grad.at[0], ret_out.at[me], load_sems.at[7])
-    own_ret.start()
+    lax.fori_loop(0, 6, band, 0)
 
     own_sum.wait()
     pltpu.make_async_copy(tail_sum, sums_out.at[core, PAIRS + chip], load_sems.at[6]).wait()
@@ -567,6 +566,10 @@
     wait_bytes(sums_out.at[core, pl.ds(0, CHIPS - 1)], tail_sems.at[5])
     swap = remote(sums_out.at[core], sums_out.at[core], swap_sems.at[0], swap_sems.at[1], lat, mate)
     swap.start()
+
+    lax.fori_loop(6, DEV // 16, band, 0)
+    own_ret = pltpu.make_async_copy(slot_grad.at[0], ret_out.at[me], load_sems.at[7])
+    own_ret.start()
     wait_bytes(bias_lon.at[pl.ds(0, CHIPS - 1)], bias_sems.at[3])
     bias_out[...] = bias_lon[...].sum(0).sum(0, keepdims=True)
 

time: 93.8 us -> 95.9 us (1.022)
  Pallas kernels: 93 us -> 94.9 us
    pallas_call x1, Pallas kernels: 87.5 us -> 89.5 us  [fused(): pl.pallas_call(kernel, out_shape=[jax.ShapeDtypeStruct((CELLS, CH), BF),...]
where the time goes in v5:
time: 95.9 us; the launch traced here: 95.7 us
  Pallas kernels  94.9 us (99%)
    pallas_call x1, Pallas kernels, fused(): pl.pallas_call(kernel, out_shape=[jax.ShapeDtypeStruct((CELLS, CH), BF),...  89.5 us
    pallas_call x1, Pallas kernels, finish(): pl.pallas_call(finish_kernel, out_shape=[jax.ShapeDtypeStruct((CELLS, CH)...  5.42 us

profile of v5, /device:TPU:1, one launch (start us, length us, event | category | flops | bytes accessed | tf_op | source)
XLA Modules:
  0.0 95.7 jit_solution(5107283617434196098)
XLA Ops:
  0.6 89.5 %fused.1 = (bf16[4096,256]{1,0:T(8,128)(2,1)}, bf16[2,72,16,256]{3,2,1,0:T(8,128)(2,1)}, bf16[128,16,256]{2,1,0:T(8,128)(2,1)}, f32[1,256]{1,0:T(1,128)}) custom-call(bf16[16,128,256]{2,1,0:T(8,128)(2,1)} %bitcast.12, f32[2,16,128]{2,1,0:T(8,128)} %bitcast.13, s32[1,128]{1,0:T(1,128)} %counts.1, s32[16,128]{1,0:T(8,128)} %bitcast.14, ...), custom_call_target="tpu_custom_call" | custom-call | tf_op jit(solution)/shard_map/fused/pallas_call | solution.py:661
  90.1 5.4 %finish.1 = (bf16[4096,256]{1,0:T(8,128)(2,1)}, f32[9,256,256]{2,1,0:T(8,128)}, f32[1,256]{1,0:T(1,128)}, bf16[16,128,256]{2,1,0:T(8,128)(2,1)}) custom-call(bf16[4096,256]{1,0:T(8,128)(2,1)} %get-tuple-element.12.enc_in, bf16[2,72,16,256]{3,2,1,0:T(8,128)(2,1)} %get-tuple-element.13.sums_in, bf16[128,16,256]{2,1,0:T(8,128)(2,1)} %get-tuple-element.14.ret_in, ...), custom_call_target="tpu_custom_call" | custom-call | tf_op jit(solution)/shard_map/finish/pallas_call | solution.py:718

commit v6 on v5

--- a/solution.py
+++ b/solution.py
@@ -558,7 +558,9 @@
         lax.fori_loop(0, 16, back, 0)
         return 0
 
-    lax.fori_loop(0, 6, band, 0)
+    lax.fori_loop(0, DEV // 16, band, 0)
+    own_ret = pltpu.make_async_copy(slot_grad.at[0], ret_out.at[me], load_sems.at[7])
+    own_ret.start()
 
     own_sum.wait()
     pltpu.make_async_copy(tail_sum, sums_out.at[core, PAIRS + chip], load_sems.at[6]).wait()
@@ -566,10 +568,6 @@
     wait_bytes(sums_out.at[core, pl.ds(0, CHIPS - 1)], tail_sems.at[5])
     swap = remote(sums_out.at[core], sums_out.at[core], swap_sems.at[0], swap_sems.at[1], lat, mate)
     swap.start()
-
-    lax.fori_loop(6, DEV // 16, band, 0)
-    own_ret = pltpu.make_async_copy(slot_grad.at[0], ret_out.at[me], load_sems.at[7])
-    own_ret.start()
     wait_bytes(bias_lon.at[pl.ds(0, CHIPS - 1)], bias_sems.at[3])
     bias_out[...] = bias_lon[...].sum(0).sum(0, keepdims=True)
 

time: 95.9 us -> 93.1 us (0.971)
  Pallas kernels: 94.9 us -> 92.1 us
    pallas_call x1, Pallas kernels: 89.5 us -> 86.7 us  [fused(): pl.pallas_call(kernel, out_shape=[jax.ShapeDtypeStruct((CELLS, CH), BF),...]
where the time goes in v6:
time: 93.1 us; the launch traced here: 92.9 us
  Pallas kernels  92.1 us (99%)
    pallas_call x1, Pallas kernels, fused(): pl.pallas_call(kernel, out_shape=[jax.ShapeDtypeStruct((CELLS, CH), BF),...  86.7 us
    pallas_call x1, Pallas kernels, finish(): pl.pallas_call(finish_kernel, out_shape=[jax.ShapeDtypeStruct((CELLS, CH)...  5.42 us

profile of v6, /device:TPU:1, one launch (start us, length us, event | category | flops | bytes accessed | tf_op | source)
XLA Modules:
  0.0 92.9 jit_solution(9024159489151001842)
XLA Ops:
  0.6 86.7 %fused.1 = (bf16[4096,256]{1,0:T(8,128)(2,1)}, bf16[2,72,16,256]{3,2,1,0:T(8,128)(2,1)}, bf16[128,16,256]{2,1,0:T(8,128)(2,1)}, f32[1,256]{1,0:T(1,128)}) custom-call(bf16[16,128,256]{2,1,0:T(8,128)(2,1)} %bitcast.12, f32[2,16,128]{2,1,0:T(8,128)} %bitcast.13, s32[1,128]{1,0:T(1,128)} %counts.1, s32[16,128]{1,0:T(8,128)} %bitcast.14, ...), custom_call_target="tpu_custom_call" | custom-call | tf_op jit(solution)/shard_map/fused/pallas_call | solution.py:659
  87.3 5.4 %finish.1 = (bf16[4096,256]{1,0:T(8,128)(2,1)}, f32[9,256,256]{2,1,0:T(8,128)}, f32[1,256]{1,0:T(1,128)}, bf16[16,128,256]{2,1,0:T(8,128)(2,1)}) custom-call(bf16[4096,256]{1,0:T(8,128)(2,1)} %get-tuple-element.12.enc_in, bf16[2,72,16,256]{3,2,1,0:T(8,128)(2,1)} %get-tuple-element.13.sums_in, bf16[128,16,256]{2,1,0:T(8,128)(2,1)} %get-tuple-element.14.ret_in, ...), custom_call_target="tpu_custom_call" | custom-call | tf_op jit(solution)/shard_map/finish/pallas_call | solution.py:716
